TPU v7x, 512 devices: a whole 4x8x8 slice. The times are simulated.
512 devices in a mesh: ctx: 32 (over y, x), tp: 16 (over z, core).
Axes of the slice: x: 4, y: 8, z: 8, core: 2. Of those that a mesh axis runs over, the one named last changes fastest.
Arguments:
- queries: bfloat16 [2048, 4096], P('ctx', 'tp'), may hold values from -6 to 6
- key_rows: bfloat16 [2048, 4096], P('ctx', 'tp'), may hold values from -6 to 6
- value_rows: bfloat16 [2048, 4096], P('ctx', 'tp'), may hold values from -6 to 6
- out_gate: bfloat16 [2048, 4096], P('ctx', 'tp'), may hold values from -9.5 to 6.5
- decay_index: int32 [32], P('tp'), may hold values from 0 to 15
- w_out: bfloat16 [4096, 3072], P('tp'), may hold values from -1 to 1
- norm_gain: float32 [3072], replicated, may hold values from 0.5 to 1.5
- expert_ids: int32 [2048, 2], P('ctx'), may hold values from 0 to 15, all different within a row; in each aligned block of 64 rows (0 to 63, 64 to 127, ...) at most 9 rows name the same one
- gate_codes: int32 [2048, 2], P('ctx'), may hold values from 1 to 1023
- w_gate: bfloat16 [32, 3072, 2304], P('ctx', None, 'tp'), may hold values from -0.109375 to 0.109375
- w_up: bfloat16 [32, 3072, 2304], P('ctx', None, 'tp'), may hold values from -0.109375 to 0.109375
- w_down: bfloat16 [32, 2304, 3072], P('ctx', 'tp'), may hold values from -0.125 to 0.125
Outputs:
- mixed: bfloat16 [2048, 3072], P('ctx', 'tp')
Inputs may be any that keep to these rules, and one draw needn't show every extreme that they name: `expert_ids`: the 2 ids of a token differ. Within the tokens of one index of ctx (aligned blocks of 64 tokens) each expert is named by at most 9 tokens, a bound that some block reaches.
All inputs are finite; a program needn't handle non-finite values.
Results may differ from a plain program's by a relative error of at most 0.015.
Values may be sent and summed in bfloat16 or wider, within the bound.
A program may use at most 64 MiB of HBM per device.

v0:
```python
import jax
import jax.numpy as jnp
from jax import lax
from jax.sharding import PartitionSpec as P

HEAD = 128
D = 3072
EXPERTS = 16
TOP = 2
NLEV = 16
CAP = 9


def carried_in(x, axis, combine, identity):
    length, index = (lax.axis_size(axis), lax.axis_index(axis))
    everything = jax.tree.map(lambda part: lax.all_gather(part, axis), x)
    start = jax.tree.map(
        lambda part, zero: jnp.broadcast_to(jnp.asarray(zero, part.dtype), part.shape), x, identity
    )

    def turn(k, before):
        reached = k < index
        new = combine(before, jax.tree.map(lambda part: part[k], everything))
        return jax.tree.map(lambda a, b: jnp.where(reached, a, b), new, before)

    return lax.fori_loop(0, length, turn, start)


def decay_rates(decay_index, seq_len):
    fraction = decay_index.astype(jnp.float32) / (NLEV - 1)
    fastest = jnp.log(jnp.float32(1.0 / 40.0))
    slowest = jnp.log(jnp.float32(1.0 / (16.0 * seq_len)))
    return jnp.exp(fastest + fraction * (slowest - fastest))


def local(
    queries,
    key_rows,
    value_rows,
    out_gate,
    decay_index,
    w_out,
    norm_gain,
    expert_ids,
    gate_codes,
    w_gate,
    w_up,
    w_down,
):
    tok_rows = queries.shape[0]
    head_count = queries.shape[1] // HEAD
    ctx_count = lax.axis_size("ctx")
    lane_count = lax.axis_size("tp")
    decays = decay_rates(decay_index, tok_rows * ctx_count)
    query_head_rows = queries.reshape(tok_rows, head_count, HEAD)
    key_head_rows = key_rows.reshape(tok_rows, head_count, HEAD)
    value_head_rows = value_rows.reshape(tok_rows, head_count, HEAD)
    places = jnp.arange(tok_rows, dtype=jnp.float32)
    offsets = places[:, None] - places[None, :]
    within = jnp.where(
        offsets[None] >= 0.0, jnp.exp(-decays[:, None, None] * jnp.maximum(offsets, 0.0)[None]), 0.0
    )
    attention_scores = jnp.einsum(
        "vkf,gkf->kvg", query_head_rows, key_head_rows, preferred_element_type=jnp.float32
    )
    routing_weights = (attention_scores * within).astype(jnp.bfloat16)
    intra_block_part = jnp.einsum(
        "brq,qbg->rbg", routing_weights, value_head_rows, preferred_element_type=jnp.float32
    )
    fading = jnp.exp(-decays[None, :] * (tok_rows - 1.0 - places)[:, None])
    local_state = jnp.einsum(
        "unz,unj->nzj",
        key_head_rows.astype(jnp.float32) * fading[:, :, None],
        value_head_rows.astype(jnp.float32),
        precision=lax.Precision.HIGHEST,
    )
    block_decay = jnp.exp(-decays * tok_rows)

    def link_states(earlier, later):
        return (earlier[0] * later[0], later[0][:, None, None] * earlier[1] + later[1])

    prefix = carried_in(
        (block_decay, local_state),
        "ctx",
        link_states,
        (jnp.ones_like(block_decay), jnp.zeros_like(local_state)),
    )
    prior_state = prefix[1]
    entering = jnp.exp(-decays[None, :] * (places + 1.0)[:, None])
    outside = (
        jnp.einsum(
            "nhd,hde->nhe",
            query_head_rows.astype(jnp.float32),
            prior_state,
            precision=lax.Precision.HIGHEST,
        )
        * entering[:, :, None]
    )
    attended = intra_block_part + outside
    inverse_scale = lax.rsqrt(jnp.mean(attended * attended, axis=2, keepdims=True) + 1e-06)
    opening = jax.nn.sigmoid(out_gate.astype(jnp.float32)).reshape(tok_rows, head_count, HEAD)
    heads_out = (
        (attended * inverse_scale * opening)
        .reshape(tok_rows, head_count * HEAD)
        .astype(jnp.bfloat16)
    )
    head_part = jnp.dot(heads_out, w_out, preferred_element_type=jnp.float32)
    lane_width = D // lane_count
    lane_start = lax.axis_index("tp") * lane_width
    residual = lax.psum_scatter(head_part, "tp", scatter_dimension=1, tiled=True)
    squares = lax.psum(jnp.sum(residual * residual, axis=1), "tp")
    row_inverse = lax.rsqrt(squares / D + 1e-05)[:, None]
    gain_here = lax.dynamic_slice_in_dim(norm_gain, lane_start, lane_width, 0)
    outgoing = (residual * row_inverse * gain_here[None, :]).astype(jnp.bfloat16)
    pair_count = tok_rows * TOP
    flat_ids = expert_ids.reshape(pair_count)
    indicator = (flat_ids[:, None] == jnp.arange(EXPERTS, dtype=jnp.int32)[None, :]).astype(
        jnp.int32
    )
    ranking = jnp.sum((jnp.cumsum(indicator, axis=0) - indicator) * indicator, axis=1)
    target = flat_ids * CAP + ranking
    slot_count = EXPERTS * CAP
    matches = target[None, :] == jnp.arange(slot_count, dtype=jnp.int32)[:, None]
    owners = jnp.sum(
        jnp.where(matches, (jnp.arange(pair_count, dtype=jnp.int32) // TOP)[None, :], 0), axis=1
    )
    filled = jnp.any(matches, axis=1)
    picked = jnp.where(
        filled[:, None], jnp.take(outgoing, owners, axis=0), jnp.zeros((), jnp.bfloat16)
    )
    doubled = jnp.repeat(picked.reshape(EXPERTS, CAP, outgoing.shape[1]), 2, axis=0)
    arrived = lax.all_to_all(doubled, "ctx", split_axis=0, concat_axis=1, tiled=True)
    pieces = lax.all_gather(arrived, "tp", axis=2, tiled=True)
    gate_sum = jnp.einsum("hrd,hdf->hrf", pieces, w_gate, preferred_element_type=jnp.float32)
    up_sum = jnp.einsum("hrd,hdf->hrf", pieces, w_up, preferred_element_type=jnp.float32)
    hidden = (jax.nn.silu(gate_sum) * up_sum).astype(jnp.bfloat16)
    partial_value = jnp.einsum(
        "hrf,hfd->hrd", hidden, w_down, preferred_element_type=jnp.float32
    ).astype(jnp.bfloat16)
    returned = lax.all_to_all(partial_value, "ctx", split_axis=1, concat_axis=0, tiled=True)
    width_back = returned.shape[2]
    flat_back = returned.reshape(2 * slot_count, width_back)
    first_half = flat_ids * (2 * CAP) + ranking
    first_rows = jnp.take(flat_back, first_half, axis=0).astype(jnp.float32)
    second_rows = jnp.take(flat_back, first_half + CAP, axis=0).astype(jnp.float32)
    routed = (first_rows + second_rows).reshape(tok_rows, TOP, width_back)
    code_values = gate_codes.astype(jnp.float32)
    shares = code_values / jnp.sum(code_values, axis=1, keepdims=True)
    moe_part = jnp.sum(routed * shares[:, :, None], axis=1)
    expert_total = lax.psum_scatter(
        moe_part.astype(jnp.bfloat16), "tp", scatter_dimension=1, tiled=True
    ).astype(jnp.float32)
    return (residual + expert_total).astype(jnp.bfloat16)


def solution(mesh):
    placed = (
        P("ctx", "tp"),
        P("ctx", "tp"),
        P("ctx", "tp"),
        P("ctx", "tp"),
        P("tp"),
        P("tp", None),
        P(),
        P("ctx", None),
        P("ctx", None),
        P("ctx", None, "tp"),
        P("ctx", None, "tp"),
        P("ctx", "tp", None),
    )
    return jax.shard_map(
        local, mesh=mesh, in_specs=placed, out_specs=P("ctx", "tp"), check_vma=False
    )
```

profile of v0, /device:TPU:1, one launch (start us, length us, event | category | flops | bytes accessed | tf_op | source)
XLA Modules:
  0.0 459.9 jit_solution(12726544819529447555)
XLA Ops:
  6.6 1.4 dynamic-slice
  9.5 1.8 fusion.31
  11.3 62.0 %all-reduce = f32[64]{0:T(128)S(1)} all-reduce(f32[64]{0:T(128)S(1)} %get-tuple-element.137), channel_id=2, replica_groups=mesh['ctx'=32,'tp'=16] {'ctx'}, use_global_device_ids=true, to_apply=%add | all-reduce | flops 64 | bytes 512
  73.5 1.0 convolution_bitcast_fusion.2
  74.5 26.9 %all-gather.7.cloned.1.call-done = f32[64,128,128]{2,1,0:T(8,128)} async-done(((f32[2,128,128]{2,1,0:T(8,128)}), f32[64,128,128]{2,1,0:T(8,128)}) %all-gather.7.cloned.1.call-update) | async-done | bytes 4194320 | tf_op jit(solution)/shard_map/all_gather | solution.py:16
  101.5 33.0 %while.14 = (s32[]{:T(128)}, f32[2,128,128]{2,1,0:T(8,128)S(1)}, s32[]{:T(128)}, f32[32,2]{1,0:T(8,128)S(1)}, f32[32,2,128,128]{3,2,1,0:T(8,128)}, /*index=5*/s32[]{:T(128)}, s32[]{:T(128)}) while((s32[]{:T(128)}, f32[2,128,128]{2,1,0:T(8,128)S(1)}, s32[]{:T(128)}, f32[32,2]{1,0:T(8,128)S(1)}, f32[32,2,128,128]{3,2,1,0:T(8,128)}, ...), condition=%wide.region_1.2_spmd.clone, body=%wide.region_0.1_spmd.clone.sunk | while | flops 131076 | bytes 393345 | solution.py:26
  102.5 1.0 fusion.76
  103.5 1.0 fusion.76
  104.6 1.0 fusion.76
  105.6 1.0 fusion.76
  107.7 1.0 fusion.76
  108.7 1.0 fusion.76
  109.7 1.0 fusion.76
  112.8 1.0 fusion.76
  113.9 1.0 fusion.76
  117.0 1.0 fusion.76
  118.0 1.0 fusion.76
  119.0 1.0 fusion.76
  122.1 1.0 fusion.76
  123.2 1.0 fusion.76
  124.2 1.0 fusion.76
  127.3 1.0 fusion.76
  128.3 1.0 fusion.76
  129.4 1.0 fusion.76
  132.5 1.0 fusion.76
  133.5 1.0 fusion.76
  134.9 1.9 convolution_bitcast_fusion
  138.8 57.2 %reduce-scatter.7.cloned.1.call-done = f32[192,64]{1,0:T(8,128)} async-done(((f32[3072,64]{1,0:T(8,128)}), f32[192,64]{1,0:T(8,128)}) %reduce-scatter.7.cloned.1.call-update) | async-done | bytes 49168
  197.1 26.5 %psum.7 = f32[64]{0:T(128)S(1)} all-reduce(f32[64]{0:T(128)S(1)} %multiply_reduce_fusion.1), channel_id=1, replica_groups=mesh['ctx'=32,'tp'=16] {'tp'}, use_global_device_ids=true, to_apply=%region_9.10 | all-reduce | flops 64 | bytes 512 | tf_op jit(solution)/shard_map/psum | solution.py:111
  225.1 18.5 %all_to_all.21 = bf16[32,2,864]{2,1,0:T(2,128)(2,1)S(1)} all-to-all(bf16[32,2,864]{2,1,0:T(2,128)(2,1)S(1)} %reshape.270), channel_id=1, replica_groups=mesh['ctx'=32,'tp'=16] {'ctx'}, dimensions={0} | all-to-all | bytes 221184 | tf_op jit(solution)/shard_map/all_to_all | solution.py:132
  244.9 42.3 %all-gather.5.cloned.1.call-done = bf16[1,288,3072]{1,0,2:T(2,128)(2,1)} async-done(((bf16[1,288,192]{1,0,2:T(2,128)(2,1)}), bf16[1,288,3072]{1,0,2:T(2,128)(2,1)}) %all-gather.5.cloned.1.call-update) | async-done | bytes 1769488 | tf_op jit(solution)/shard_map/all_gather | solution.py:133
  287.2 10.8 %copy.62 = bf16[1,288,3072]{2,1,0:T(8,128)(2,1)S(1)} copy(bf16[1,288,3072]{1,0,2:T(2,128)(2,1)} %all-gather.5.cloned.1.call-done) | data formatting | bytes 3538944 | tf_op jit(solution)/shard_map/all_gather | solution.py:133
  297.9 2.7 fusion.4
  300.7 4.7 %fusion.1 = bf16[1,288,3072]{2,1,0:T(8,128)(2,1)} fusion(bf16[1,144,3072]{2,1,0:T(8,128)(2,1)} %param.27, bf16[1,288,3072]{2,1,0:T(8,128)(2,1)S(1)} %copy.62, bf16[1,3072,144]{1,2,0:T(8,128)(2,1)} %param.26, f32[288,144]{0,1:T(8,128)} %fusion.4), kind=kOutput, calls=%fused_computation.7 | convolution fusion | flops 510741504 | bytes 5474304 | tf_op jit(solution)/shard_map/hrf,hfd->hrd/dot_general | solution.py:137
  305.3 6.0 %copy.115 = bf16[1,288,3072]{2,0,1:T(2,128)(2,1)} copy(bf16[1,288,3072]{2,1,0:T(8,128)(2,1)} %fusion.1) | data formatting | bytes 3538944 | tf_op jit(solution)/shard_map/convert_element_type | solution.py:139
  311.8 11.6 %reduce = bf16[288,3072]{1,0:T(8,128)(2,1)S(1)} reduce(bf16[288,1,3072]{2,1,0:T(2,128)(2,1)} %bitcast.127, bf16[]{:T(256)} %broadcast.212), dimensions={1}, to_apply=%bitcast.120.reduce_sub_computation | reduce | bytes 3538946
  323.4 2.1 reshape.272
  325.5 9.4 %all-to-all-start.1 = ((bf16[32,2,13824]{2,1,0:T(2,128)(2,1)}), bf16[32,2,13824]{2,1,0:T(2,128)(2,1)S(1)}, u32[]{:S(2)}, u32[]{:S(2)}) async-start(bf16[32,2,13824]{2,1,0:T(2,128)(2,1)} %reshape.272), calls=%async_computation.1 | async-start | bytes 3538944 | tf_op jit(solution)/shard_map/all_to_all | solution.py:140
  335.3 41.2 %all-to-all-done.1 = bf16[32,2,13824]{2,1,0:T(2,128)(2,1)S(1)} async-done(((bf16[32,2,13824]{2,1,0:T(2,128)(2,1)}), bf16[32,2,13824]{2,1,0:T(2,128)(2,1)S(1)}, u32[]{:S(2)}, u32[]{:S(2)}) %all-to-all-start.1) | async-done | bytes 1769504 | tf_op jit(solution)/shard_map/all_to_all | solution.py:140
  376.6 6.2 %reshape.273 = bf16[288,1,3072]{2,1,0:T(2,128)(2,1)} reshape(bf16[32,2,13824]{2,1,0:T(2,128)(2,1)S(1)} %all-to-all-done.1) | data formatting | bytes 3538944
  382.8 2.5 copy.114
  385.3 1.9 gather_fusion.1
  387.3 1.9 gather_fusion.2
  389.2 1.8 convert_add_fusion
  391.0 2.1 reshape.228
  393.1 3.6 multiply_reduce_fusion
  396.7 1.2 copy.67
  397.8 54.0 %reduce-scatter.9.cloned.1.call-done = bf16[192,64]{1,0:T(8,128)(2,1)} async-done(((bf16[3072,64]{1,0:T(8,128)(2,1)}), bf16[192,64]{1,0:T(8,128)(2,1)}) %reduce-scatter.9.cloned.1.call-update) | async-done | bytes 24592
  (106 shorter events, 21.8 us)
Async XLA Ops:
  6.5 128.3 %copy-start = (bf16[256,3072]{1,0:T(8,128)(2,1)S(1)}, bf16[256,3072]{1,0:T(8,128)(2,1)}, u32[]{:S(2)}) copy-start(bf16[256,3072]{1,0:T(8,128)(2,1)} %param.21) | copy-start | bytes 4718596
  6.5 128.0 %copy-start.2 = (bf16[64,256]{1,0:T(8,128)(2,1)S(1)}, bf16[64,256]{1,0:T(8,128)(2,1)}, u32[]{:S(2)}) copy-start(bf16[64,256]{1,0:T(8,128)(2,1)} %param.16) | copy-start | bytes 98308
  6.5 128.3 %copy-start.1 = (bf16[64,256]{1,0:T(8,128)(2,1)S(1)}, bf16[64,256]{1,0:T(8,128)(2,1)}, u32[]{:S(2)}) copy-start(bf16[64,256]{1,0:T(8,128)(2,1)} %param.19) | copy-start | bytes 98308
  6.5 94.9 %all-gather.7.cloned.1.call-start = ((), (), s32[]{:S(2)}) async-start(), calls=%async_computation.5 | async-start | bytes 4325376 | tf_op jit(solution)/shard_map/all_gather | solution.py:16
  11.3 184.8 %reduce-scatter.7.cloned.1.call-start = ((), (), s32[]{:S(2)}) async-start(), calls=%async_computation.6 | async-start | bytes 1671168
  134.8 2.0 copy-start.3
  136.8 150.3 %all-gather.5.cloned.1.call-start = ((), (), s32[]{:S(2)}) async-start(), calls=%async_computation.4 | async-start | bytes 5013504 | tf_op jit(solution)/shard_map/all_gather | solution.py:133
  325.5 9.7 %copy-start.4 = (s32[64,2]{0,1:T(2,128)S(1)}, s32[64,2]{0,1:T(2,128)}, u32[]{:S(2)}) copy-start(s32[64,2]{0,1:T(2,128)} %param.24) | copy-start | bytes 1540
  325.5 51.1 %all-to-all-start.1 = ((bf16[32,2,13824]{2,1,0:T(2,128)(2,1)}), bf16[32,2,13824]{2,1,0:T(2,128)(2,1)S(1)}, u32[]{:S(2)}, u32[]{:S(2)}) async-start(bf16[32,2,13824]{2,1,0:T(2,128)(2,1)} %reshape.272), calls=%async_computation.1 | async-start | bytes 3538944 | tf_op jit(solution)/shard_map/all_to_all | solution.py:140
  334.9 117.0 %reduce-scatter.9.cloned.1.call-start = ((), (), s32[]{:S(2)}) async-start(), calls=%async_computation.7 | async-start | bytes 835584
Sparse Core Ops, SparseCore 0:
  11.4 90.0 all-gather.6
  136.9 59.0 reduce-scatter.6
  245.0 42.1 all-gather.4
  398.0 53.8 reduce-scatter.8
where the time goes:
time: 464 us; the launch traced here: 460 us
  waiting for transfers between devices  222 us (48%)
  blocking collectives  107 us (23%)
  other arithmetic  51.3 us (11%)
  local copies, waits for them, and re-layouts  42.7 us (9%)
  between operations  14.1 us (3%)
  matrix products  12.4 us (3%)
  starting transfers between devices  9.74 us (2%)
    unnamed x6, waiting for transfers between devices  111 us
    unnamed x1, blocking collectives  62 us
    all_gather x1, waiting for transfers between devices, local(): pieces = lax.all_gather(arrived, 'tp', axis=2, tiled=True)  42.3 us
    all_to_all x1, waiting for transfers between devices, local(): lax.all_to_all(partial_value, 'ctx', split_axis=1, concat_axis=0, tiled=T...  41.2 us
    select_n x32, other arithmetic, turn(): return jax.tree.map(lambda a, b: jnp.where(reached, a, b), new, before)  31.8 us
    all_gather x1, waiting for transfers between devices, carried_in(): everything = jax.tree.map(lambda part: lax.all_gather(part, axis), x)  26.9 us
    psum x1, blocking collectives, local(): squares = lax.psum(jnp.sum(residual * residual, axis=1), 'tp')  26.5 us
    all_to_all x1, blocking collectives, local(): lax.all_to_all(doubled, 'ctx', split_axis=0, concat_axis=1, tiled=True)  18.5 us
  transfers between devices with their start and end apart: 5, of which 5 were waited for; matrix products, arithmetic and copies ran while one was open for 1% of the time, Pallas kernels for 0%

commit v1 on v0

v1 whole, which is shorter than its diff:
```python
import functools

import jax
import jax.numpy as jnp
from jax import lax
from jax.experimental import pallas as pl
from jax.experimental.pallas import tpu as pltpu
from jax.sharding import PartitionSpec as P

HEAD = 128
TOP = 2
NLEV = 16
CAP = 9
TOK = 64
HALF = TOK // 2
SLAB = 384
LANE = 128
TILES = SLAB // LANE
MSG = 32
UNITS = 144
MESH = pl.DeviceIdType.MESH
BF = jnp.bfloat16
F32 = jnp.float32


def mm(a, b):
    return jnp.dot(a, b, preferred_element_type=F32)


def mm_t(a, b):
    return lax.dot_general(a, b, (((0,), (0,)), ((), ())), preferred_element_type=F32)


def wait_bytes(ref, sem):
    pltpu.make_async_copy(ref, ref, sem).wait()


def iota(shape, dim):
    return lax.broadcasted_iota(jnp.int32, shape, dim)


def kernel(
    C,
    NT,
    TOKENS,
    idx_ref,
    q_ref,
    k_ref,
    v_ref,
    og_ref,
    gain_ref,
    ids_ref,
    codes_ref,
    wout_hbm,
    wg_hbm,
    wu_hbm,
    wd_hbm,
    out_ref,
    wout_v,
    wg_v,
    wu_v,
    wd_v,
    state_v,
    win_v,
    pst_v,
    prior_v,
    ho_v,
    hs_v,
    rst_v,
    rsb_v,
    pick_v,
    comb_v,
    res_v,
    mst_v,
    arr_v,
    x_v,
    sp_v,
    rp_v,
    m2_v,
    ret_v,
    fin_v,
    wl_sem,
    ws_sem,
    wr_sem,
    one_send,
    one_recv,
    ag_send,
    ag_recv,
    rs_send,
    rs_recv,
):
    NZ = NT // 2
    H = NZ // 2
    E = C // 2
    PR = 2 * HEAD // E
    RQ = x_v.shape[1]
    D = NZ * SLAB
    first = (RQ // 16 + 1) // 2 * 16
    parts = ((0, first), (first, RQ - first))

    c = lax.axis_index("ctx")
    t = lax.axis_index("tp")
    z = lax.div(t, 2)
    core = lax.rem(t, 2)
    sib = t + 1 - 2 * core
    side = lax.rem(c, 2)
    mine = lax.div(c, 2)
    active = side == core

    ST1, ST2, HO, RS, DISP, RETN, FIN = range(7)

    def put(src, dst, send, recv, ctx, tp):
        pltpu.make_async_remote_copy(
            src_ref=src,
            dst_ref=dst,
            send_sem=send,
            recv_sem=recv,
            device_id={"ctx": ctx, "tp": tp},
            device_id_type=MESH,
        ).start()

    barrier = pltpu.get_barrier_semaphore()

    def greet_ctx(i, carry):
        pl.semaphore_signal(
            barrier, inc=1, device_id={"ctx": lax.rem(c + i, C), "tp": t}, device_id_type=MESH
        )
        return carry

    def greet_tp(i, carry):
        pl.semaphore_signal(
            barrier, inc=1, device_id={"ctx": c, "tp": lax.rem(t + i, NT)}, device_id_type=MESH
        )
        return carry

    lax.fori_loop(1, C, greet_ctx, 0)
    lax.fori_loop(1, NT, greet_tp, 0)

    weights = (
        (wout_hbm, wout_v),
        (wg_hbm.at[0], wg_v),
        (wu_hbm.at[0], wu_v),
        (wd_hbm.at[0], wd_v),
    )
    for n, (src, dst) in enumerate(weights):
        pltpu.make_async_copy(src, dst.at[0], wl_sem.at[n]).start()

    log_fast = jnp.log(jnp.full((1, 1), 1.0 / 40.0, F32))
    log_slow = jnp.log(jnp.full((1, 1), 1.0 / (16.0 * TOKENS), F32))
    rates = []
    for h in range(2):
        fraction = jnp.full((1, 1), idx_ref[h].astype(F32), F32) / (NLEV - 1)
        rates.append(jnp.exp(log_fast + fraction * (log_slow - log_fast)))
    place = iota((TOK, 1), 0).astype(F32)
    for h in range(2):
        cols = slice(h * HEAD, (h + 1) * HEAD)
        fading = jnp.exp(-rates[h] * (TOK - 1.0 - place))
        faded = (k_ref[:, cols].astype(F32) * fading).astype(BF)
        state = mm_t(faded, v_ref[:, cols]).astype(BF)
        each = HEAD // PR
        state_v[h * each : (h + 1) * each] = state.reshape(each, PR, HEAD)

    pl.semaphore_wait(barrier, C - 1 + NT - 1)

    def send_piece(i, carry):
        j = lax.rem(mine + i, E)
        put(
            state_v.at[j], win_v.at[c], one_send.at[ST1], one_recv.at[ST1], 2 * j + core, t
        )
        return carry

    lax.fori_loop(1, E, send_piece, 0)

    @pl.when(jnp.logical_not(active))
    def _():
        send_piece(0, 0)

    for n, (src, dst) in enumerate(weights):
        put(src, dst.at[1], ws_sem.at[n], wr_sem.at[n], c, sib)

    n_at, m_at = iota((TOK, TOK), 0), iota((TOK, TOK), 1)
    offsets = (n_at - m_at).astype(F32)
    inside = []
    for h in range(2):
        cols = slice(h * HEAD, (h + 1) * HEAD)
        scores = lax.dot_general(
            q_ref[:, cols], k_ref[:, cols], (((1,), (1,)), ((), ())), preferred_element_type=F32
        )
        within = jnp.where(
            offsets >= 0.0, jnp.exp(-rates[h] * jnp.maximum(offsets, 0.0)), 0.0
        )
        inside.append(mm((scores * within).astype(BF), v_ref[:, cols]))

    @pl.when(active)
    def _():
        win_v[c] = state_v[mine]
        wait_bytes(win_v.at[pl.ds(0, C - 1)], one_recv.at[ST1])
        first_head = mine * PR < HEAD
        decay = jnp.exp(-jnp.where(first_head, rates[0], rates[1]) * TOK)

        def turn(b, run):
            pst_v[b] = run.astype(BF)
            return run * decay + win_v[b].astype(F32)

        lax.fori_loop(0, C, turn, jnp.zeros((PR, HEAD), F32), unroll=True)
        prior_v[mine] = pst_v[c]

        def send_prefix(i, carry):
            to = lax.rem(c + i, C)
            put(pst_v.at[to], prior_v.at[mine], one_send.at[ST2], one_recv.at[ST2], to, t)
            return carry

        lax.fori_loop(1, C, send_prefix, 0)

    @pl.when(active)
    def _():
        ids = ids_ref[...].astype(F32)
        codes = codes_ref[...].astype(F32)
        share = codes / jnp.sum(codes, axis=1, keepdims=True)
        expert_at = iota((TOK, LANE), 1).astype(F32)
        hot = [jnp.where(expert_at == ids[:, j : j + 1], 1.0, 0.0) for j in range(TOP)]
        before = jnp.where(n_at > m_at, 1.0, 0.0).astype(BF)
        count = mm(before, (hot[0] + hot[1]).astype(BF))
        rank = [jnp.sum(hot[j] * count, axis=1, keepdims=True) for j in range(TOP)]
        row_at = iota((TOK, E * MSG), 1).astype(F32)
        both_at = iota((TOK, C * MSG), 1)
        both_at = (both_at - MSG * lax.rem(lax.div(both_at, MSG), 2)).astype(F32)
        for l in range(TILES):
            out_row = [MSG * ids[:, j : j + 1] + rank[j] + CAP * l for j in range(TOP)]
            taken = (row_at == out_row[0]) | (row_at == out_row[1])
            pick_v[l * TOK : (l + 1) * TOK] = jnp.where(taken, 1.0, 0.0).astype(BF)
            back_row = [2 * MSG * ids[:, j : j + 1] + rank[j] + CAP * l for j in range(TOP)]
            comb_v[l] = (
                jnp.where(both_at == back_row[0], share[:, 0:1], 0.0)
                + jnp.where(both_at == back_row[1], share[:, 1:2], 0.0)
            ).astype(BF)

    @pl.when(active)
    def _():
        wait_bytes(prior_v.at[pl.ds(0, E - 1)], one_recv.at[ST2])

    @pl.when(jnp.logical_not(active))
    def _():
        wait_bytes(prior_v, one_recv.at[ST2])

    prior = prior_v[...].reshape(2 * HEAD, HEAD)
    for h in range(2):
        cols = slice(h * HEAD, (h + 1) * HEAD)
        entering = jnp.exp(-rates[h] * (place + 1.0))
        attended = inside[h] + mm(q_ref[:, cols], prior[h * HEAD : (h + 1) * HEAD]) * entering
        scale = lax.rsqrt(jnp.mean(attended * attended, axis=1, keepdims=True) + 1e-06)
        opening = jax.nn.sigmoid(og_ref[:, cols].astype(F32))
        ho_v[:, cols] = (attended * scale * opening).astype(BF)

    other_rows = pl.multiple_of(HALF * (1 - core), HALF)
    my_rows = pl.multiple_of(HALF * core, HALF)
    put(ho_v.at[pl.ds(other_rows, HALF)], hs_v, one_send.at[HO], one_recv.at[HO], c, sib)
    heads_here = ho_v[pl.ds(my_rows, HALF)]
    pltpu.make_async_copy(wout_hbm, wout_v.at[0], wl_sem.at[0]).wait()
    wait_bytes(wout_v.at[1], wr_sem.at[0])
    wait_bytes(hs_v, one_recv.at[HO])
    heads_there = hs_v[...]

    lead = 2 * z + side
    order = sorted(range(NZ), key=lambda i: -min(i, NZ - i))
    for i in order:
        zz = lax.rem(z + i, NZ)
        cols = pl.ds(pl.multiple_of(zz * SLAB, SLAB), SLAB)
        part = mm(heads_here, wout_v[0, :, cols]) + mm(heads_there, wout_v[1, :, cols])
        rst_v[i] = part.astype(BF)
        if i:
            put(rst_v.at[i], rsb_v.at[t], one_send.at[RS], one_recv.at[RS], c, 2 * zz + side)

    @pl.when(jnp.logical_not(active))
    def _():
        put(rst_v.at[0], rsb_v.at[t], one_send.at[RS], one_recv.at[RS], c, lead)

    @pl.when(active)
    def _():
        rsb_v[t] = rst_v[0]
        wait_bytes(rsb_v.at[pl.ds(0, NT - 1)], one_recv.at[RS])
        gain = gain_ref[pl.ds(pl.multiple_of(z * SLAB, SLAB), SLAB)].reshape(1, SLAB)
        for half in range(2):
            total = rsb_v[half].astype(F32)
            for zz in range(1, NZ):
                total = total + rsb_v[2 * zz + half].astype(F32)
            res_v[half * HALF : (half + 1) * HALF] = total
        scaled = (res_v[...] * gain).astype(BF)
        message = jnp.zeros((E * MSG, LANE), F32)
        for l in range(TILES):
            message = message + mm_t(
                pick_v[l * TOK : (l + 1) * TOK], scaled[:, l * LANE : (l + 1) * LANE]
            )
        mst_v[...] = message.astype(BF).reshape(E, MSG, LANE)

        def send_rows(i, carry):
            to = lax.rem(c + i, C)
            put(
                mst_v.at[lax.div(to, 2)],
                arr_v.at[mine],
                one_send.at[DISP],
                one_recv.at[DISP],
                to,
                t,
            )
            return carry

        lax.fori_loop(1, C, send_rows, 0)
        arr_v[mine] = mst_v[mine]
        wait_bytes(arr_v.at[pl.ds(0, E - 1)], one_recv.at[DISP])

    @pl.when(jnp.logical_not(active))
    def _():
        wait_bytes(arr_v, one_recv.at[DISP])

    arrived = arr_v[...].reshape(E * MSG, LANE)
    slot_row, at = iota((RQ, E * MSG), 0), iota((RQ, E * MSG), 1)
    slot_row = MSG * lax.div(slot_row, CAP) + lax.rem(slot_row, CAP)
    for l in range(TILES):
        spread = jnp.where(at == slot_row + CAP * l, 1.0, 0.0).astype(BF)
        x_v[z, :, l * LANE : (l + 1) * LANE] = mm(spread, arrived).astype(BF)

    def at_z(step):
        return lax.rem(z + step + 2 * NZ, NZ)

    def carried(step, way):
        return (way,) if step == H else (0, 1)

    def pass_on(step, way):
        turn = 1 if way == 0 else -1
        chunk = at_z(-turn * (step - 1))
        for p in carried(step, way):
            begin, size = parts[p]
            if step > 1:
                wait_bytes(
                    x_v.at[chunk, pl.ds(begin, size)], ag_recv.at[way, step - 2, p]
                )
            put(
                x_v.at[chunk, pl.ds(begin, size)],
                x_v.at[chunk, pl.ds(begin, size)],
                ag_send.at[way, step - 1, p],
                ag_recv.at[way, step - 1, p],
                c,
                2 * at_z(turn) + core,
            )

    def take(chunk, totals):
        x = x_v[chunk]
        rows = pl.ds(pl.multiple_of(chunk * SLAB, SLAB), SLAB)
        gain = gain_ref[rows].reshape(1, SLAB)
        wide = x.astype(F32) / gain
        squares = jnp.sum(wide * wide, axis=1, keepdims=True)
        new = [squares]
        for i in range(2):
            new.append(mm(x, wg_v[i, rows]))
            new.append(mm(x, wu_v[i, rows]))
        return [a + b for a, b in zip(totals, new)] if totals else new

    for way in range(2):
        pass_on(1, way)
    for n in (1, 2):
        src, dst = weights[n]
        pltpu.make_async_copy(src, dst.at[0], wl_sem.at[n]).wait()
        wait_bytes(dst.at[1], wr_sem.at[n])
    totals = take(z, None)
    for step in range(1, H + 1):
        for way in range(2):
            if step < H:
                pass_on(step + 1, way)
        for way in range(2):
            turn = 1 if way == 0 else -1
            chunk = at_z(-turn * step)
            gone = carried(step + 1, way) if step < H else ()
            for p in carried(step, way):
                if p not in gone:
                    begin, size = parts[p]
                    wait_bytes(
                        x_v.at[chunk, pl.ds(begin, size)], ag_recv.at[way, step - 1, p]
                    )
            if step < H:
                totals = take(chunk, totals)
        if step == H:
            totals = take(at_z(H), totals)

    inverse = lax.rsqrt(totals[0] / D + 1e-05)
    hidden = []
    for i in range(2):
        gate = totals[1 + 2 * i] * inverse
        up = totals[2 + 2 * i] * inverse
        hidden.append((jax.nn.silu(gate) * up).astype(BF))

    src, dst = weights[3]
    pltpu.make_async_copy(src, dst.at[0], wl_sem.at[3]).wait()
    wait_bytes(dst.at[1], wr_sem.at[3])

    def down(chunk):
        cols = pl.ds(pl.multiple_of(chunk * SLAB, SLAB), SLAB)
        return mm(hidden[0], wd_v[0, :, cols]) + mm(hidden[1], wd_v[1, :, cols])

    for step in range(1, H + 1):
        if step == 1:
            far = down(at_z(H))
            values = (far, far)
        else:
            values = (down(at_z(H + 1 - step)), down(at_z(-(H + 1 - step))))
        for way in range(2):
            turn = 1 if way == 0 else -1
            for p in (way,) if step == 1 else (way, 1 - way):
                begin, size = parts[p]
                value = values[way][begin : begin + size]
                if step > 2 or (step == 2 and p == way):
                    wait_bytes(
                        rp_v.at[way, step - 2, pl.ds(begin, size)],
                        rs_recv.at[way, step - 2, p],
                    )
                    value = value + rp_v[way, step - 2, pl.ds(begin, size)].astype(F32)
                sp_v[way, step - 1, pl.ds(begin, size)] = value.astype(BF)
                put(
                    sp_v.at[way, step - 1, pl.ds(begin, size)],
                    rp_v.at[way, step - 1, pl.ds(begin, size)],
                    rs_send.at[way, step - 1, p],
                    rs_recv.at[way, step - 1, p],
                    c,
                    2 * at_z(turn) + core,
                )
    own = down(z)
    pieces = []
    for p in range(2):
        begin, size = parts[p]
        value = own[begin : begin + size]
        for way in range(2):
            if H > 1 or p == way:
                wait_bytes(
                    rp_v.at[way, H - 1, pl.ds(begin, size)], rs_recv.at[way, H - 1, p]
                )
                value = value + rp_v[way, H - 1, pl.ds(begin, size)].astype(F32)
        pieces.append(value.astype(BF))
    final = jnp.concatenate(pieces, axis=0)

    slot_col, at = iota((E * MSG, RQ), 1), iota((E * MSG, RQ), 0)
    slot_col = MSG * lax.div(slot_col, CAP) + lax.rem(slot_col, CAP)
    message = jnp.zeros((E * MSG, LANE), F32)
    for l in range(TILES):
        gather = jnp.where(at == slot_col + CAP * l, 1.0, 0.0).astype(BF)
        message = message + mm(gather, final[:, l * LANE : (l + 1) * LANE])
    m2_v[...] = message.astype(BF).reshape(E, MSG, LANE)

    def send_back(i, carry):
        j = lax.rem(mine + i, E)
        put(m2_v.at[j], ret_v.at[c], one_send.at[RETN], one_recv.at[RETN], 2 * j + core, t)
        return carry

    lax.fori_loop(1, E, send_back, 0)

    @pl.when(jnp.logical_not(active))
    def _():
        send_back(0, 0)

    width = out_ref.shape[1]

    @pl.when(active)
    def _():
        ret_v[c] = m2_v[mine]
        wait_bytes(ret_v.at[pl.ds(0, C - 1)], one_recv.at[RETN])
        returned = ret_v[...].reshape(C * MSG, LANE)
        moe = jnp.concatenate([mm(comb_v[l], returned) for l in range(TILES)], axis=1)
        mixed = res_v[...] + moe
        low, high = mixed[:, :width].astype(BF), mixed[:, width:].astype(BF)
        fin_v[...] = jnp.where(core == 0, high, low)
        put(fin_v, out_ref, one_send.at[FIN], one_recv.at[FIN], c, sib)
        out_ref[...] = jnp.where(core == 0, low, high)

    @pl.when(active)
    def _():
        wait_bytes(state_v.at[pl.ds(0, E - 1)], one_send.at[ST1])
        wait_bytes(pst_v.at[pl.ds(0, C - 1)], one_send.at[ST2])
        wait_bytes(rst_v.at[pl.ds(0, NZ - 1)], one_send.at[RS])
        for _ in range(2):
            wait_bytes(mst_v.at[pl.ds(0, E - 1)], one_send.at[DISP])
        wait_bytes(mst_v.at[0], one_send.at[DISP])
        wait_bytes(m2_v.at[pl.ds(0, E - 1)], one_send.at[RETN])
        wait_bytes(fin_v, one_send.at[FIN])

    @pl.when(jnp.logical_not(active))
    def _():
        wait_bytes(state_v, one_send.at[ST1])
        wait_bytes(rst_v, one_send.at[RS])
        wait_bytes(m2_v, one_send.at[RETN])
        wait_bytes(out_ref, one_recv.at[FIN])

    wait_bytes(hs_v, one_send.at[HO])
    for n, (src, dst) in enumerate(weights):
        wait_bytes(dst.at[1], ws_sem.at[n])
    for way in range(2):
        for step in range(1, H + 1):
            for p in carried(step, way):
                begin, size = parts[p]
                wait_bytes(x_v.at[0, pl.ds(begin, size)], ag_send.at[way, step - 1, p])
            for p in (way,) if step == 1 else (0, 1):
                begin, size = parts[p]
                wait_bytes(
                    sp_v.at[way, step - 1, pl.ds(begin, size)], rs_send.at[way, step - 1, p]
                )


def local(C, NT, tokens, *args):
    (queries, key_rows, value_rows, out_gate, decay_index, w_out, norm_gain,
     expert_ids, gate_codes, w_gate, w_up, w_down) = args
    NZ = NT // 2
    H = NZ // 2
    E = C // 2
    PR = 2 * HEAD // E
    RQ = -(-E * CAP // 16) * 16
    D = NZ * SLAB
    vmem = pl.BlockSpec(memory_space=pltpu.VMEM)
    hbm = pl.BlockSpec(memory_space=pl.ANY)
    dma = pltpu.SemaphoreType.DMA
    return pl.pallas_call(
        functools.partial(kernel, C, NT, tokens),
        out_shape=jax.ShapeDtypeStruct((TOK, SLAB // 2), BF),
        in_specs=[pl.BlockSpec(memory_space=pltpu.SMEM)] + [vmem] * 7 + [hbm] * 4,
        out_specs=vmem,
        scratch_shapes=[
            pltpu.VMEM((2, 2 * HEAD, D), BF),
            pltpu.VMEM((2, D, UNITS), BF),
            pltpu.VMEM((2, D, UNITS), BF),
            pltpu.VMEM((2, UNITS, D), BF),
            pltpu.VMEM((E, PR, HEAD), BF),
            pltpu.VMEM((C, PR, HEAD), BF),
            pltpu.VMEM((C, PR, HEAD), BF),
            pltpu.VMEM((E, PR, HEAD), BF),
            pltpu.VMEM((TOK, 2 * HEAD), BF),
            pltpu.VMEM((HALF, 2 * HEAD), BF),
            pltpu.VMEM((NZ, HALF, SLAB), BF),
            pltpu.VMEM((NT, HALF, SLAB), BF),
            pltpu.VMEM((TILES * TOK, E * MSG), BF),
            pltpu.VMEM((TILES, TOK, C * MSG), BF),
            pltpu.VMEM((TOK, SLAB), F32),
            pltpu.VMEM((E, MSG, LANE), BF),
            pltpu.VMEM((E, MSG, LANE), BF),
            pltpu.VMEM((NZ, RQ, SLAB), BF),
            pltpu.VMEM((2, H, RQ, SLAB), BF),
            pltpu.VMEM((2, H, RQ, SLAB), BF),
            pltpu.VMEM((E, MSG, LANE), BF),
            pltpu.VMEM((C, MSG, LANE), BF),
            pltpu.VMEM((TOK, SLAB // 2), BF),
            dma((4,)),
            dma((4,)),
            dma((4,)),
            dma((7,)),
            dma((7,)),
            dma((2, H, 2)),
            dma((2, H, 2)),
            dma((2, H, 2)),
            dma((2, H, 2)),
        ],
        compiler_params=pltpu.CompilerParams(
            collective_id=0, has_side_effects=True, vmem_limit_bytes=48 * 2**20
        ),
        cost_estimate=pl.CostEstimate(
            flops=1_000_000_000, bytes_accessed=8_000_000, transcendentals=100_000
        ),
        name="layer",
    )(
        decay_index,
        queries,
        key_rows,
        value_rows,
        out_gate,
        norm_gain,
        expert_ids,
        gate_codes,
        w_out,
        w_gate,
        w_up,
        w_down,
    )


def solution(mesh):
    C, NT = mesh.shape["ctx"], mesh.shape["tp"]
    placed = (
        P("ctx", "tp"),
        P("ctx", "tp"),
        P("ctx", "tp"),
        P("ctx", "tp"),
        P("tp"),
        P("tp", None),
        P(),
        P("ctx", None),
        P("ctx", None),
        P("ctx", None, "tp"),
        P("ctx", None, "tp"),
        P("ctx", "tp", None),
    )

    def whole(*args):
        tokens = args[0].shape[0]
        return jax.shard_map(
            functools.partial(local, C, NT, tokens),
            mesh=mesh,
            in_specs=placed,
            out_specs=P("ctx", "tp"),
            check_vma=False,
        )(*args)

    return whole
```

time: 464 us -> 96.5 us (0.21)
  waiting for transfers between devices: 222 us -> 0 us
  blocking collectives: 107 us -> 0 us
  Pallas kernels: 0 us -> 88.2 us
  other arithmetic: 51.3 us -> 0 us
  local copies, waits for them, and re-layouts: 42.7 us -> 7.95 us
  between operations: 14.1 us -> 0.13 us
  matrix products: 12.4 us -> 0 us
  starting transfers between devices: 9.74 us -> 0 us
    unnamed x6 -> x0, waiting for transfers between devices: 111 us -> none
    pallas_call x0 -> x1, Pallas kernels: none -> 88.2 us  [local(): pl.pallas_call(functools.partial(kernel, C, NT, tokens), out_shape=jax.Sh...]
    all_gather x2 -> x0, waiting for transfers between devices: 69.2 us -> none  [the longest x1 42.3 us: local(): pieces = lax.all_gather(arrived, 'tp', axis=2, tiled=True)]
    unnamed x1 -> x0, blocking collectives: 62 us -> none
    all_to_all x1 -> x0, waiting for transfers between devices: 41.2 us -> none  [local(): lax.all_to_all(partial_value, 'ctx', split_axis=1, concat_axis=0, tiled=T...]
    select_n x35 -> x0, other arithmetic: 31.9 us -> none  [the longest x32 31.8 us: turn(): return jax.tree.map(lambda a, b: jnp.where(reached, a, b), new, before)]
    psum x1 -> x0, blocking collectives: 26.5 us -> none  [local(): squares = lax.psum(jnp.sum(residual * residual, axis=1), 'tp')]
    all_to_all x1 -> x0, blocking collectives: 18.5 us -> none  [local(): lax.all_to_all(doubled, 'ctx', split_axis=0, concat_axis=1, tiled=True)]
  transfers between devices with their start and end apart: 5 -> 0, of which waited for: 5 -> 0; matrix products, arithmetic and copies ran while one was open for 1% -> 0% of each run, Pallas kernels for 0% -> 0%
where the time goes in v1:
time: 96.5 us; the launch traced here: 96.3 us
  Pallas kernels  88.2 us (91%)
  local copies, waits for them, and re-layouts  7.95 us (8%)
    pallas_call x1, Pallas kernels, local(): pl.pallas_call(functools.partial(kernel, C, NT, tokens), out_shape=jax.Sh...  88.2 us
    unnamed x21, local copies, waits for them, and re-layouts  7.95 us

profile of v1, /device:TPU:1, one launch (start us, length us, event | category | flops | bytes accessed | tf_op | source)
XLA Modules:
  0.0 96.3 jit_solution(657511197739789203)
XLA Ops:
  0.0 0.8 copy.13.ids_ref
  0.8 0.8 copy.14.codes_ref
  1.5 1.6 %copy.15.wg_hbm = bf16[1,3072,144]{2,1,0:T(8,128)(2,1)S(1)} copy(bf16[1,3072,144]{1,2,0:T(8,128)(2,1)} %param.21) | data formatting | bytes 1769472 | tf_op args[9]
  3.1 0.0 copy-start.2
  3.1 0.0 copy-start.3
  3.1 0.0 copy-start.4
  3.2 0.0 copy-start.5
  3.2 0.0 copy-start.6
  3.2 0.0 copy-start.7
  3.2 1.6 %copy.16.wu_hbm = bf16[1,3072,144]{2,1,0:T(8,128)(2,1)S(1)} copy(bf16[1,3072,144]{1,2,0:T(8,128)(2,1)} %param.22) | data formatting | bytes 1769472 | tf_op args[10]
  4.8 0.0 copy-done.2
  4.8 0.0 copy-done.3
  4.8 0.0 copy-done.4
  4.8 0.0 copy-done.5
  4.9 0.0 copy-done.6
  4.9 0.0 copy-done.7
  4.9 0.0 copy-start
  4.9 1.4 %copy-done = bf16[256,3072]{1,0:T(8,128)(2,1)S(1)} copy-done((bf16[256,3072]{1,0:T(8,128)(2,1)S(1)}, bf16[256,3072]{1,0:T(8,128)(2,1)}, u32[]{:S(2)}) %copy-start) | copy-done | bytes 1572888
  6.3 0.0 copy-start.1
  6.3 1.2 %copy-done.1 = bf16[1,144,3072]{2,1,0:T(8,128)(2,1)S(1)} copy-done((bf16[1,144,3072]{2,1,0:T(8,128)(2,1)S(1)}, bf16[1,144,3072]{2,1,0:T(8,128)(2,1)}, u32[]{:S(2)}) %copy-start.1) | copy-done | bytes 884760
  7.5 88.2 %layer.1 = bf16[64,192]{1,0:T(8,128)(2,1)S(1)} custom-call(s32[2]{0:T(128)S(1)} %copy-done.7, bf16[64,256]{1,0:T(8,128)(2,1)S(1)} %copy-done.2, bf16[64,256]{1,0:T(8,128)(2,1)S(1)} %copy-done.3, bf16[64,256]{1,0:T(8,128)(2,1)S(1)} %copy-done.4, bf16[64,256]{1,0:T(8,128)(2,1)S(1)} %copy-done.5, f32[3072]{0:T(1024)S(1)} %copy-done.6, ...), custom_call_target="tpu_custom_call" | custom-call | flops 1000000000 | bytes 8000000 | tf_op jit(solution)/shard_map/layer/pallas_call | solution.py:518
  95.7 0.6 copy.18
Async XLA Ops:
  3.1 1.7 %copy-start.2 = (bf16[64,256]{1,0:T(8,128)(2,1)S(1)}, bf16[64,256]{1,0:T(8,128)(2,1)}, u32[]{:S(2)}) copy-start(bf16[64,256]{1,0:T(8,128)(2,1)} %q_ref.1) | copy-start | bytes 98308
  3.1 1.7 %copy-start.3 = (bf16[64,256]{1,0:T(8,128)(2,1)S(1)}, bf16[64,256]{1,0:T(8,128)(2,1)}, u32[]{:S(2)}) copy-start(bf16[64,256]{1,0:T(8,128)(2,1)} %k_ref.1) | copy-start | bytes 98308
  3.1 1.7 %copy-start.4 = (bf16[64,256]{1,0:T(8,128)(2,1)S(1)}, bf16[64,256]{1,0:T(8,128)(2,1)}, u32[]{:S(2)}) copy-start(bf16[64,256]{1,0:T(8,128)(2,1)} %v_ref.1) | copy-start | bytes 98308
  3.2 1.7 %copy-start.5 = (bf16[64,256]{1,0:T(8,128)(2,1)S(1)}, bf16[64,256]{1,0:T(8,128)(2,1)}, u32[]{:S(2)}) copy-start(bf16[64,256]{1,0:T(8,128)(2,1)} %og_ref.1) | copy-start | bytes 98308
  3.2 1.7 %copy-start.6 = (f32[3072]{0:T(1024)S(1)}, f32[3072]{0:T(1024)}, u32[]{:S(2)}) copy-start(f32[3072]{0:T(1024)} %gain_ref.1) | copy-start | bytes 36868
  3.2 1.7 %copy-start.7 = (s32[2]{0:T(128)S(1)}, s32[2]{0:T(128)}, u32[]{:S(2)}) copy-start(s32[2]{0:T(128)} %idx_ref.1) | copy-start | bytes 28
  4.9 1.4 %copy-start = (bf16[256,3072]{1,0:T(8,128)(2,1)S(1)}, bf16[256,3072]{1,0:T(8,128)(2,1)}, u32[]{:S(2)}) copy-start(bf16[256,3072]{1,0:T(8,128)(2,1)} %wout_hbm.1) | copy-start | bytes 4718596
  6.3 1.2 %copy-start.1 = (bf16[1,144,3072]{2,1,0:T(8,128)(2,1)S(1)}, bf16[1,144,3072]{2,1,0:T(8,128)(2,1)}, u32[]{:S(2)}) copy-start(bf16[1,144,3072]{2,1,0:T(8,128)(2,1)} %wd_hbm.1) | copy-start | bytes 2654212

commit v2 on v1

v2 whole, which is shorter than its diff:
```python
import functools

import jax
import jax.numpy as jnp
from jax import lax
from jax.experimental import pallas as pl
from jax.experimental.pallas import tpu as pltpu
from jax.sharding import PartitionSpec as P

HEAD = 128
TOP = 2
NLEV = 16
CAP = 9
TOK = 64
SLAB = 384
LANE = 128
TILES = SLAB // LANE
MSG = 32
UNITS = 144
WIDE = 256
PARTS = 3
NX = 4
MESH = pl.DeviceIdType.MESH
BF = jnp.bfloat16
F32 = jnp.float32


def mm(a, b):
    return jnp.dot(a, b, preferred_element_type=F32)


def mm_t(a, b):
    return lax.dot_general(a, b, (((0,), (0,)), ((), ())), preferred_element_type=F32)


def mm_nt(a, b):
    return lax.dot_general(a, b, (((1,), (1,)), ((), ())), preferred_element_type=F32)


def wait_bytes(ref, sem):
    pltpu.make_async_copy(ref, ref, sem).wait()


def iota(shape, dim):
    return lax.broadcasted_iota(jnp.int32, shape, dim)


def kernel(
    C,
    NT,
    TOKENS,
    idx_ref,
    q_hbm,
    k_hbm,
    v_hbm,
    og_hbm,
    gain_hbm,
    ids_hbm,
    codes_hbm,
    wout_hbm,
    wg_hbm,
    wu_hbm,
    wd_hbm,
    out_ref,
    q_ref,
    k_ref,
    v_ref,
    og_ref,
    gain_ref,
    ids_ref,
    codes_ref,
    wout_v,
    w1_v,
    wd_v,
    state_v,
    win_v,
    pst_v,
    prior_v,
    open_v,
    inside_v,
    ho_v,
    hs_v,
    rst_v,
    rsb_v,
    pick_v,
    comb_v,
    res_v,
    mst_v,
    arr_v,
    spread_v,
    gather_v,
    x_v,
    sum_v,
    square_v,
    sp_v,
    rp_v,
    m2_v,
    ret_v,
    fin_v,
    in_sem,
    wl_sem,
    ws_sem,
    wr_sem,
    one_send,
    one_recv,
    ag_send,
    ag_recv,
    rs_send,
    rs_recv,
):
    NZ = NT // 2
    H = NZ // 2
    E = C // 2
    PR = 2 * HEAD // E
    RQ = x_v.shape[1]
    D = NZ * SLAB
    NY = C // NX
    units = RQ // 16
    count = min(PARTS, units)
    edges = [16 * (units * p // count) for p in range(count + 1)]
    parts = [(a, b - a) for a, b in zip(edges, edges[1:])]
    split = (count + 1) // 2

    c = lax.axis_index("ctx")
    t = lax.axis_index("tp")
    z = lax.div(t, 2)
    core = lax.rem(t, 2)
    sib = t + 1 - 2 * core
    side = lax.rem(c, 2)
    mine = lax.div(c, 2)
    active = side == core
    idle = jnp.logical_not(active)
    y_at = lax.div(c, NX)
    x_at = lax.rem(c, NX)

    def away(k, n):
        half = lax.div(k + 1, 2)
        return lax.rem(n // 2 + jnp.where(lax.rem(k, 2) == 1, n - half, half), n)

    def everyone(i):
        to_y = lax.rem(y_at + away(lax.div(i, NX), NY), NY)
        return NX * to_y + lax.rem(x_at + away(lax.rem(i, NX), NX), NX)

    def pairs(i):
        hop = NX // 2 - 1 - lax.rem(i, NX // 2)
        to_y = lax.rem(y_at + away(lax.div(i, NX // 2), NY), NY)
        return NX // 2 * to_y + lax.rem(lax.div(x_at, 2) + hop, NX // 2)

    ST1, ST2, HO, RS, PAIR, DISP, RETN, FIN = range(8)

    def put(src, dst, send, recv, ctx, tp):
        pltpu.make_async_remote_copy(
            src_ref=src,
            dst_ref=dst,
            send_sem=send,
            recv_sem=recv,
            device_id={"ctx": ctx, "tp": tp},
            device_id_type=MESH,
        ).start()

    drains = []

    def later(ref, sem, when=None):
        drains.append((ref, sem, when))

    def finish():
        for ref, sem, when in drains:
            if when is None:
                wait_bytes(ref, sem)
            else:
                pl.when(when)(functools.partial(wait_bytes, ref, sem))

    inputs = (
        (k_hbm, k_ref),
        (v_hbm, v_ref),
        (q_hbm, q_ref),
        (og_hbm, og_ref),
        (ids_hbm, ids_ref),
        (codes_hbm, codes_ref),
        (gain_hbm, gain_ref),
    )
    loads = [
        pltpu.make_async_copy(src, dst, in_sem.at[n]) for n, (src, dst) in enumerate(inputs)
    ]
    for load in loads:
        load.start()

    barrier = pltpu.get_barrier_semaphore()

    def greet_ctx(i, carry):
        pl.semaphore_signal(
            barrier, inc=1, device_id={"ctx": everyone(i), "tp": t}, device_id_type=MESH
        )
        return carry

    def greet_tp(i, carry):
        pl.semaphore_signal(
            barrier, inc=1, device_id={"ctx": c, "tp": lax.rem(t + i, NT)}, device_id_type=MESH
        )
        return carry

    lax.fori_loop(0, C - 1, greet_ctx, 0)
    lax.fori_loop(1, NT, greet_tp, 0)

    def rows_of(ref, n):
        return ref.at[pl.ds(n * UNITS, UNITS)]

    weights = (
        (wout_hbm, wout_v.at[0], wout_v.at[1]),
        (wg_hbm.at[0], rows_of(w1_v, 0), rows_of(w1_v, 1)),
        (wu_hbm.at[0], rows_of(w1_v, 2), rows_of(w1_v, 3)),
        (wd_hbm.at[0], rows_of(wd_v, 0), rows_of(wd_v, 1)),
    )
    for n, (src, here, there) in enumerate(weights):
        pltpu.make_async_copy(src, here, wl_sem.at[n]).start()

    def have(n):
        src, here, there = weights[n]
        pltpu.make_async_copy(src, here, wl_sem.at[n]).wait()
        wait_bytes(there, wr_sem.at[n])

    log_fast = jnp.log(jnp.full((1, 1), 1.0 / 40.0, F32))
    log_slow = jnp.log(jnp.full((1, 1), 1.0 / (16.0 * TOKENS), F32))
    rates = []
    for h in range(2):
        fraction = jnp.full((1, 1), idx_ref[h].astype(F32), F32) / (NLEV - 1)
        rates.append(jnp.exp(log_fast + fraction * (log_slow - log_fast)))
    place = iota((TOK, 1), 0).astype(F32)
    loads[0].wait()
    loads[1].wait()
    for h in range(2):
        cols = slice(h * HEAD, (h + 1) * HEAD)
        fading = jnp.exp(-rates[h] * (TOK - 1.0 - place))
        faded = (k_ref[:, cols].astype(F32) * fading).astype(BF)
        state = mm_t(faded, v_ref[:, cols]).astype(BF)
        each = HEAD // PR
        state_v[h * each : (h + 1) * each] = state.reshape(each, PR, HEAD)

    pl.semaphore_wait(barrier, C - 1 + NT - 1)

    def send_piece(i, carry):
        j = pairs(i)
        put(
            state_v.at[j], win_v.at[c], one_send.at[ST1], one_recv.at[ST1], 2 * j + core, t
        )
        return carry

    lax.fori_loop(0, E - 1, send_piece, 0)

    @pl.when(idle)
    def _():
        send_piece(E - 1, 0)

    later(state_v.at[pl.ds(0, E - 1)], one_send.at[ST1], active)
    later(state_v, one_send.at[ST1], idle)
    for n, (src, here, there) in enumerate(weights):
        put(src, there, ws_sem.at[n], wr_sem.at[n], c, sib)
        later(there, ws_sem.at[n])

    for load in loads[2:]:
        load.wait()
    n_at, m_at = iota((TOK, TOK), 0), iota((TOK, TOK), 1)
    offsets = (n_at - m_at).astype(F32)
    for h in range(2):
        cols = slice(h * HEAD, (h + 1) * HEAD)
        scores = mm_nt(q_ref[:, cols], k_ref[:, cols])
        within = jnp.where(
            offsets >= 0.0, jnp.exp(-rates[h] * jnp.maximum(offsets, 0.0)), 0.0
        )
        inside_v[:, cols] = mm((scores * within).astype(BF), v_ref[:, cols])
    open_v[...] = jax.nn.sigmoid(og_ref[...].astype(F32))

    @pl.when(active)
    def _():
        win_v[c] = state_v[mine]
        wait_bytes(win_v.at[pl.ds(0, C - 1)], one_recv.at[ST1])
        first_head = mine * PR < HEAD
        decay = jnp.exp(-jnp.where(first_head, rates[0], rates[1]) * TOK)

        def turn(b, run):
            pst_v[b] = run.astype(BF)
            return run * decay + win_v[b].astype(F32)

        lax.fori_loop(0, C, turn, jnp.zeros((PR, HEAD), F32), unroll=True)

        def send_prefix(i, carry):
            to = everyone(i)
            put(pst_v.at[to], prior_v.at[mine], one_send.at[ST2], one_recv.at[ST2], to, t)
            return carry

        lax.fori_loop(0, C - 1, send_prefix, 0)
        prior_v[mine] = pst_v[c]

    later(pst_v.at[pl.ds(0, C - 1)], one_send.at[ST2], active)

    @pl.when(active)
    def _():
        eye = n_at == m_at

        def stand(row):
            return jnp.sum(jnp.where(eye, row, 0.0), axis=1, keepdims=True)

        def lie(column):
            return jnp.sum(jnp.where(eye, column, 0.0), axis=0, keepdims=True)

        ids = [stand(ids_ref[j : j + 1].astype(F32)) for j in range(TOP)]
        codes = [codes_ref[j : j + 1].astype(F32) for j in range(TOP)]
        share = [stand(codes[j] / (codes[0] + codes[1])) for j in range(TOP)]
        expert_at = iota((TOK, LANE), 1).astype(F32)
        hot = [jnp.where(expert_at == ids[j], 1.0, 0.0) for j in range(TOP)]
        before = jnp.where(n_at > m_at, 1.0, 0.0).astype(BF)
        ahead = mm(before, (hot[0] + hot[1]).astype(BF))
        rank = [jnp.sum(hot[j] * ahead, axis=1, keepdims=True) for j in range(TOP)]
        out_row = [lie(MSG * ids[j] + rank[j]) for j in range(TOP)]
        back_row = [2 * MSG * ids[j] + rank[j] for j in range(TOP)]
        row_at = iota((E * MSG, TOK), 0).astype(F32)
        both_at = iota((TOK, C * MSG), 1)
        both_at = (both_at - MSG * lax.rem(lax.div(both_at, MSG), 2)).astype(F32)
        for l in range(TILES):
            taken = (row_at == out_row[0] + CAP * l) | (row_at == out_row[1] + CAP * l)
            pick_v[:, l * TOK : (l + 1) * TOK] = jnp.where(taken, 1.0, 0.0).astype(BF)
            comb_v[l * TOK : (l + 1) * TOK] = (
                jnp.where(both_at == back_row[0] + CAP * l, share[0], 0.0)
                + jnp.where(both_at == back_row[1] + CAP * l, share[1], 0.0)
            ).astype(BF)

    slot_row, at = iota((RQ, E * MSG), 0), iota((RQ, E * MSG), 1)
    slot_row = MSG * lax.div(slot_row, CAP) + lax.rem(slot_row, CAP)
    for l in range(TILES):
        spread_v[l * RQ : (l + 1) * RQ] = jnp.where(at == slot_row + CAP * l, 1.0, 0.0).astype(BF)
    slot_col, at = iota((E * MSG, RQ), 1), iota((E * MSG, RQ), 0)
    slot_col = MSG * lax.div(slot_col, CAP) + lax.rem(slot_col, CAP)
    for l in range(TILES):
        gather_v[l] = jnp.where(at == slot_col + CAP * l, 1.0, 0.0).astype(BF)

    pl.when(active)(
        functools.partial(wait_bytes, prior_v.at[pl.ds(0, E - 1)], one_recv.at[ST2])
    )
    pl.when(idle)(functools.partial(wait_bytes, prior_v, one_recv.at[ST2]))
    prior = prior_v[...].reshape(2 * HEAD, HEAD)
    for h in range(2):
        cols = slice(h * HEAD, (h + 1) * HEAD)
        entering = jnp.exp(-rates[h] * (place + 1.0))
        attended = (
            inside_v[:, cols] + mm(q_ref[:, cols], prior[h * HEAD : (h + 1) * HEAD]) * entering
        )
        scale = lax.rsqrt(jnp.mean(attended * attended, axis=1, keepdims=True) + 1e-06)
        ho_v[:, cols] = (attended * scale * open_v[:, cols]).astype(BF)

    put(ho_v, hs_v, one_send.at[HO], one_recv.at[HO], c, sib)
    later(hs_v, one_send.at[HO])
    have(0)
    wait_bytes(hs_v, one_recv.at[HO])

    lead = 2 * z + side
    order = sorted(range(NZ), key=lambda i: -min(i, NZ - i))

    def project(begin, size):
        lanes = pl.ds(begin, size)
        for i in order:
            zz = lax.rem(z + i, NZ)
            cols = pl.ds(pl.multiple_of(zz * SLAB, SLAB) + begin, size)
            part = mm(ho_v[...], wout_v[0, :, cols]) + mm(hs_v[...], wout_v[1, :, cols])
            rst_v[i, :, :size] = part.astype(BF)
            if i:
                put(
                    rst_v.at[i, :, pl.ds(0, size)],
                    rsb_v.at[z, :, lanes],
                    one_send.at[RS],
                    one_recv.at[RS],
                    c,
                    2 * zz + side,
                )

        @pl.when(idle)
        def _():
            put(
                rst_v.at[0, :, pl.ds(0, size)],
                rsb_v.at[z, :, lanes],
                one_send.at[PAIR],
                one_recv.at[PAIR],
                c,
                lead,
            )

        @pl.when(active)
        def _():
            rsb_v[z, :, begin : begin + size] = rst_v[0, :, :size]

    for k, (begin, size) in enumerate(((0, WIDE), (WIDE, SLAB - WIDE))):
        here = core == k
        pl.when(here)(functools.partial(project, begin, size))
        later(rst_v.at[pl.ds(0, NZ - 1), :, pl.ds(0, size)], one_send.at[RS], here)
        later(rst_v.at[0, :, pl.ds(0, size)], one_send.at[PAIR], here & idle)

    @pl.when(active)
    def _():
        for k, size in enumerate((SLAB - WIDE, WIDE)):
            pl.when(core == k)(
                functools.partial(
                    wait_bytes, rsb_v.at[0, :, pl.ds(0, size)], one_recv.at[PAIR]
                )
            )
        wait_bytes(rsb_v.at[pl.ds(0, NZ - 1)], one_recv.at[RS])
        gain = gain_ref[pl.ds(pl.multiple_of(z * SLAB, SLAB), SLAB)].reshape(1, SLAB)
        total = rsb_v[0].astype(F32)
        for zz in range(1, NZ):
            total = total + rsb_v[zz].astype(F32)
        res_v[...] = total
        scaled = (total * gain).astype(BF)
        stacked = jnp.concatenate(
            [scaled[:, l * LANE : (l + 1) * LANE] for l in range(TILES)], axis=0
        )
        mst_v[...] = mm(pick_v[...], stacked).astype(BF).reshape(E, MSG, LANE)

        def send_rows(i, carry):
            to = everyone(i)
            put(
                mst_v.at[lax.div(to, 2)],
                arr_v.at[mine],
                one_send.at[DISP],
                one_recv.at[DISP],
                to,
                t,
            )
            return carry

        lax.fori_loop(0, C - 1, send_rows, 0)
        arr_v[mine] = mst_v[mine]
        wait_bytes(arr_v.at[pl.ds(0, E - 1)], one_recv.at[DISP])

    pl.when(idle)(functools.partial(wait_bytes, arr_v, one_recv.at[DISP]))
    for _ in range(2):
        later(mst_v.at[pl.ds(0, E - 1)], one_send.at[DISP], active)
    later(mst_v.at[0], one_send.at[DISP], active)

    spread = mm(spread_v[...], arr_v[...].reshape(E * MSG, LANE)).astype(BF)
    for l in range(TILES):
        x_v[z, :, l * LANE : (l + 1) * LANE] = spread[l * RQ : (l + 1) * RQ]

    def at_z(step):
        return lax.rem(z + step + 2 * NZ, NZ)

    def carried(step, way):
        if step < H:
            return range(count)
        return range(split) if way == 0 else range(split, count)

    def pass_on(step, way, p):
        turn = 1 - 2 * way
        begin, size = parts[p]
        piece = x_v.at[at_z(-turn * (step - 1)), pl.ds(begin, size)]
        put(
            piece,
            piece,
            ag_send.at[way, step - 1, p],
            ag_recv.at[way, step - 1, p],
            c,
            2 * at_z(turn) + core,
        )
        later(piece, ag_send.at[way, step - 1, p])

    def take(step):
        chunk = at_z(step)
        rows = pl.ds(pl.multiple_of(chunk * SLAB, SLAB), SLAB)
        x = x_v[chunk]
        new = mm_nt(x, w1_v[:, rows])
        wide = x.astype(F32) / gain_ref[rows].reshape(1, SLAB)
        wide = wide * wide
        squares = wide[:, :LANE]
        for l in range(1, TILES):
            squares = squares + wide[:, l * LANE : (l + 1) * LANE]
        if step == 0:
            sum_v[...] = new
            square_v[...] = squares
        else:
            sum_v[...] += new
            square_v[...] += squares

    for p in range(count):
        for way in range(2):
            if p in carried(1, way):
                pass_on(1, way, p)
    have(1)
    have(2)
    ready = [0]
    for step in range(1, H + 1):
        for p in range(count):
            for way in range(2):
                if p in carried(step, way):
                    begin, size = parts[p]
                    wait_bytes(
                        x_v.at[at_z((2 * way - 1) * step), pl.ds(begin, size)],
                        ag_recv.at[way, step - 1, p],
                    )
                    if step < H and p in carried(step + 1, way):
                        pass_on(step + 1, way, p)
            if ready:
                take(ready.pop(0))
        while ready:
            take(ready.pop(0))
        ready = [-step, step] if step < H else [H]
    take(H)

    inverse = lax.rsqrt(jnp.sum(square_v[...], axis=1, keepdims=True) / D + 1e-05)
    gate = sum_v[:, : 2 * UNITS] * inverse
    up = sum_v[:, 2 * UNITS :] * inverse
    hidden = (jax.nn.silu(gate) * up).astype(BF)
    have(3)

    def down(step):
        cols = pl.ds(pl.multiple_of(at_z(step) * SLAB, SLAB), SLAB)
        return mm(hidden, wd_v[:, cols])

    for step in range(1, H + 1):
        if step == 1:
            far = down(H)
            values = (far, far)
        else:
            values = (down(H + 1 - step), down(-(H + 1 - step)))
        for p in range(count):
            begin, size = parts[p]
            piece = pl.ds(begin, size)
            for way in range(2):
                if step == 1 and p not in carried(H, way):
                    continue
                value = values[way][begin : begin + size]
                if step > 2 or (step == 2 and p in carried(H, way)):
                    wait_bytes(rp_v.at[way, step - 2, piece], rs_recv.at[way, step - 2, p])
                    value = value + rp_v[way, step - 2, piece].astype(F32)
                sp_v[way, step - 1, piece] = value.astype(BF)
                put(
                    sp_v.at[way, step - 1, piece],
                    rp_v.at[way, step - 1, piece],
                    rs_send.at[way, step - 1, p],
                    rs_recv.at[way, step - 1, p],
                    c,
                    2 * at_z(1 - 2 * way) + core,
                )
                later(sp_v.at[way, step - 1, piece], rs_send.at[way, step - 1, p])
    own = down(0)
    pieces = []
    for p in range(count):
        begin, size = parts[p]
        piece = pl.ds(begin, size)
        value = own[begin : begin + size]
        for way in range(2):
            if H > 1 or p in carried(H, way):
                wait_bytes(rp_v.at[way, H - 1, piece], rs_recv.at[way, H - 1, p])
                value = value + rp_v[way, H - 1, piece].astype(F32)
        pieces.append(value.astype(BF))
    final = jnp.concatenate(pieces, axis=0)

    message = jnp.zeros((E * MSG, LANE), F32)
    for l in range(TILES):
        message = message + mm(gather_v[l], final[:, l * LANE : (l + 1) * LANE])
    m2_v[...] = message.astype(BF).reshape(E, MSG, LANE)

    def send_back(i, carry):
        j = pairs(i)
        put(m2_v.at[j], ret_v.at[c], one_send.at[RETN], one_recv.at[RETN], 2 * j + core, t)
        return carry

    lax.fori_loop(0, E - 1, send_back, 0)

    @pl.when(idle)
    def _():
        send_back(E - 1, 0)

    later(m2_v.at[pl.ds(0, E - 1)], one_send.at[RETN], active)
    later(m2_v, one_send.at[RETN], idle)
    width = out_ref.shape[1]

    @pl.when(active)
    def _():
        ret_v[c] = m2_v[mine]
        wait_bytes(ret_v.at[pl.ds(0, C - 1)], one_recv.at[RETN])
        tall = mm(comb_v[...], ret_v[...].reshape(C * MSG, LANE))
        moe = jnp.concatenate([tall[l * TOK : (l + 1) * TOK] for l in range(TILES)], axis=1)
        mixed = res_v[...] + moe
        low, high = mixed[:, :width].astype(BF), mixed[:, width:].astype(BF)
        fin_v[...] = jnp.where(core == 0, high, low)
        put(fin_v, out_ref, one_send.at[FIN], one_recv.at[FIN], c, sib)
        out_ref[...] = jnp.where(core == 0, low, high)

    later(fin_v, one_send.at[FIN], active)
    later(out_ref, one_recv.at[FIN], idle)
    finish()


def local(C, NT, tokens, *args):
    (queries, key_rows, value_rows, out_gate, decay_index, w_out, norm_gain,
     expert_ids, gate_codes, w_gate, w_up, w_down) = args
    NZ = NT // 2
    H = NZ // 2
    E = C // 2
    PR = 2 * HEAD // E
    RQ = -(-E * CAP // 16) * 16
    D = NZ * SLAB
    vmem = pl.BlockSpec(memory_space=pltpu.VMEM)
    hbm = pl.BlockSpec(memory_space=pltpu.HBM)
    dma = pltpu.SemaphoreType.DMA
    return pl.pallas_call(
        functools.partial(kernel, C, NT, tokens),
        out_shape=jax.ShapeDtypeStruct((TOK, SLAB // 2), BF),
        in_specs=[pl.BlockSpec(memory_space=pltpu.SMEM)] + [hbm] * 11,
        out_specs=vmem,
        scratch_shapes=[
            pltpu.VMEM((TOK, 2 * HEAD), BF),
            pltpu.VMEM((TOK, 2 * HEAD), BF),
            pltpu.VMEM((TOK, 2 * HEAD), BF),
            pltpu.VMEM((TOK, 2 * HEAD), BF),
            pltpu.VMEM((D,), F32),
            pltpu.VMEM((TOP, TOK), jnp.int32),
            pltpu.VMEM((TOP, TOK), jnp.int32),
            pltpu.VMEM((2, 2 * HEAD, D), BF),
            pltpu.VMEM((4 * UNITS, D), BF),
            pltpu.VMEM((2 * UNITS, D), BF),
            pltpu.VMEM((E, PR, HEAD), BF),
            pltpu.VMEM((C, PR, HEAD), BF),
            pltpu.VMEM((C, PR, HEAD), BF),
            pltpu.VMEM((E, PR, HEAD), BF),
            pltpu.VMEM((TOK, 2 * HEAD), F32),
            pltpu.VMEM((TOK, 2 * HEAD), F32),
            pltpu.VMEM((TOK, 2 * HEAD), BF),
            pltpu.VMEM((TOK, 2 * HEAD), BF),
            pltpu.VMEM((NZ, TOK, WIDE), BF),
            pltpu.VMEM((NZ, TOK, SLAB), BF),
            pltpu.VMEM((E * MSG, TILES * TOK), BF),
            pltpu.VMEM((TILES * TOK, C * MSG), BF),
            pltpu.VMEM((TOK, SLAB), F32),
            pltpu.VMEM((E, MSG, LANE), BF),
            pltpu.VMEM((E, MSG, LANE), BF),
            pltpu.VMEM((TILES * RQ, E * MSG), BF),
            pltpu.VMEM((TILES, E * MSG, RQ), BF),
            pltpu.VMEM((NZ, RQ, SLAB), BF),
            pltpu.VMEM((RQ, 4 * UNITS), F32),
            pltpu.VMEM((RQ, LANE), F32),
            pltpu.VMEM((2, H, RQ, SLAB), BF),
            pltpu.VMEM((2, H, RQ, SLAB), BF),
            pltpu.VMEM((E, MSG, LANE), BF),
            pltpu.VMEM((C, MSG, LANE), BF),
            pltpu.VMEM((TOK, SLAB // 2), BF),
            dma((7,)),
            dma((4,)),
            dma((4,)),
            dma((4,)),
            dma((8,)),
            dma((8,)),
            dma((2, H, PARTS)),
            dma((2, H, PARTS)),
            dma((2, H, PARTS)),
            dma((2, H, PARTS)),
        ],
        compiler_params=pltpu.CompilerParams(
            collective_id=0, has_side_effects=True, vmem_limit_bytes=60 * 2**20
        ),
        cost_estimate=pl.CostEstimate(
            flops=1_000_000_000, bytes_accessed=8_000_000, transcendentals=100_000
        ),
        name="layer",
    )(
        decay_index,
        queries,
        key_rows,
        value_rows,
        out_gate,
        norm_gain,
        expert_ids.T,
        gate_codes.T,
        w_out,
        w_gate.transpose(0, 2, 1),
        w_up.transpose(0, 2, 1),
        w_down,
    )


def solution(mesh):
    C, NT = mesh.shape["ctx"], mesh.shape["tp"]
    placed = (
        P("ctx", "tp"),
        P("ctx", "tp"),
        P("ctx", "tp"),
        P("ctx", "tp"),
        P("tp"),
        P("tp", None),
        P(),
        P("ctx", None),
        P("ctx", None),
        P("ctx", None, "tp"),
        P("ctx", None, "tp"),
        P("ctx", "tp", None),
    )

    def whole(*args):
        tokens = args[0].shape[0]
        return jax.shard_map(
            functools.partial(local, C, NT, tokens),
            mesh=mesh,
            in_specs=placed,
            out_specs=P("ctx", "tp"),
            check_vma=False,
        )(*args)

    return whole
```

time: 96.5 us -> 87.5 us (0.907)
  local copies, waits for them, and re-layouts: 7.95 us -> 1.38 us
  Pallas kernels: 88.2 us -> 85.9 us
    unnamed x21 -> x1, local copies, waits for them, and re-layouts: 7.95 us -> 1.38 us
    pallas_call x1, Pallas kernels: 88.2 us -> 85.9 us  [local(): pl.pallas_call(functools.partial(kernel, C, NT, tokens), out_shape=jax.Sh...]
where the time goes in v2:
time: 87.5 us; the launch traced here: 87.3 us
  Pallas kernels  85.9 us (98%)
  local copies, waits for them, and re-layouts  1.38 us (2%)
    pallas_call x1, Pallas kernels, local(): pl.pallas_call(functools.partial(kernel, C, NT, tokens), out_shape=jax.Sh...  85.9 us

profile of v2, /device:TPU:1, one launch (start us, length us, event | category | flops | bytes accessed | tf_op | source)
XLA Modules:
  0.0 87.3 jit_solution(4925795298873032888)
XLA Ops:
  0.0 85.9 %layer.1 = bf16[64,192]{1,0:T(8,128)(2,1)} custom-call(s32[2]{0:T(128)} %idx_ref.1, bf16[64,256]{1,0:T(8,128)(2,1)} %q_hbm.1, bf16[64,256]{1,0:T(8,128)(2,1)} %k_hbm.1, bf16[64,256]{1,0:T(8,128)(2,1)} %v_hbm.1, bf16[64,256]{1,0:T(8,128)(2,1)} %og_hbm.1, f32[3072]{0:T(1024)} %gain_hbm.1, s32[2,64]{1,0:T(2,128)} %bitcast.6, s32[2,64]{1,0:T(2,128)} %bitcast.7, ...), custom_call_target="tpu_custom_call" | custom-call | flops 1000000000 | bytes 8000000 | tf_op jit(solution)/shard_map/layer/pallas_call | solution.py:603
  85.9 1.4 %copy.14 = bf16[64,192]{1,0:T(8,128)(2,1)} copy(bf16[64,192]{1,0:T(8,128)(2,1)} %layer.1) | data formatting | bytes 49152

commit v3 on v2

--- a/solution.py
+++ b/solution.py
@@ -18,7 +18,7 @@
 MSG = 32
 UNITS = 144
 WIDE = 256
-PARTS = 3
+PARTS = 4
 NX = 4
 MESH = pl.DeviceIdType.MESH
 BF = jnp.bfloat16
@@ -78,6 +78,7 @@
     prior_v,
     open_v,
     inside_v,
+    enter_v,
     ho_v,
     hs_v,
     rst_v,
@@ -92,6 +93,8 @@
     x_v,
     sum_v,
     square_v,
+    hidden_v,
+    last_v,
     sp_v,
     rp_v,
     m2_v,
@@ -103,6 +106,7 @@
     wr_sem,
     one_send,
     one_recv,
+    disp_recv,
     ag_send,
     ag_recv,
     rs_send,
@@ -120,6 +124,9 @@
     edges = [16 * (units * p // count) for p in range(count + 1)]
     parts = [(a, b - a) for a, b in zip(edges, edges[1:])]
     split = (count + 1) // 2
+    begins = [e // CAP for e in edges[:-1]]
+    reach = [0] + [min(E, -(-e // CAP)) for e in edges[1:]]
+    whole = [0] + [min(E, e // CAP) for e in edges[1:]]
 
     c = lax.axis_index("ctx")
     t = lax.axis_index("tp")
@@ -146,6 +153,21 @@
         to_y = lax.rem(y_at + away(lax.div(i, NX // 2), NY), NY)
         return NX // 2 * to_y + lax.rem(lax.div(x_at, 2) + hop, NX // 2)
 
+    def slot_at(to):
+        far = lax.rem(y_at - lax.div(to, NX) + NY, NY)
+        rank = jnp.where(
+            far == 0, 0, jnp.where(far <= NY // 2, 2 * far - 1, 2 * (NY - far))
+        )
+        return NX // 2 * rank + lax.div(x_at, 2)
+
+    def block_of(slot):
+        rank = lax.div(slot, NX // 2)
+        half = lax.div(rank + 1, 2)
+        far = jnp.where(lax.rem(rank, 2) == 1, half, NY - half)
+        return NX * lax.rem(y_at + far, NY) + core + 2 * lax.rem(slot, NX // 2)
+
+    own_slot = lax.div(x_at, 2)
+
     ST1, ST2, HO, RS, PAIR, DISP, RETN, FIN = range(8)
 
     def put(src, dst, send, recv, ctx, tp):
@@ -169,6 +191,7 @@
                 wait_bytes(ref, sem)
             else:
                 pl.when(when)(functools.partial(wait_bytes, ref, sem))
+        drains.clear()
 
     inputs = (
         (k_hbm, k_ref),
@@ -269,6 +292,13 @@
         )
         inside_v[:, cols] = mm((scores * within).astype(BF), v_ref[:, cols])
     open_v[...] = jax.nn.sigmoid(og_ref[...].astype(F32))
+    enter_v[...] = jnp.concatenate(
+        [
+            jnp.broadcast_to(jnp.exp(-rates[h] * (place + 1.0)), (TOK, HEAD))
+            for h in range(2)
+        ],
+        axis=1,
+    )
 
     @pl.when(active)
     def _():
@@ -324,14 +354,26 @@
                 + jnp.where(both_at == back_row[1] + CAP * l, share[1], 0.0)
             ).astype(BF)
 
-    slot_row, at = iota((RQ, E * MSG), 0), iota((RQ, E * MSG), 1)
-    slot_row = MSG * lax.div(slot_row, CAP) + lax.rem(slot_row, CAP)
-    for l in range(TILES):
-        spread_v[l * RQ : (l + 1) * RQ] = jnp.where(at == slot_row + CAP * l, 1.0, 0.0).astype(BF)
-    slot_col, at = iota((E * MSG, RQ), 1), iota((E * MSG, RQ), 0)
-    slot_col = MSG * lax.div(slot_col, CAP) + lax.rem(slot_col, CAP)
-    for l in range(TILES):
-        gather_v[l] = jnp.where(at == slot_col + CAP * l, 1.0, 0.0).astype(BF)
+    for p, (begin, size) in enumerate(parts):
+        deep = MSG * (reach[p + 1] - begins[p])
+        if deep:
+            row, at = begin + iota((size, deep), 0), iota((size, deep), 1)
+            row = MSG * (lax.div(row, CAP) - begins[p]) + lax.rem(row, CAP)
+            for l in range(TILES):
+                start = TILES * begin + l * size
+                spread_v[start : start + size, :deep] = jnp.where(
+                    at == row + CAP * l, 1.0, 0.0
+                ).astype(BF)
+        low, high = whole[p], whole[p + 1]
+        if low < high:
+            base = CAP * low // 16 * 16
+            shape = (MSG * (high - low), edges[p + 1] - base)
+            at, row = MSG * low + iota(shape, 0), base + iota(shape, 1)
+            row = MSG * lax.div(row, CAP) + lax.rem(row, CAP)
+            for l in range(TILES):
+                gather_v[l, MSG * low : MSG * high, : shape[1]] = jnp.where(
+                    at == row + CAP * l, 1.0, 0.0
+                ).astype(BF)
 
     pl.when(active)(
         functools.partial(wait_bytes, prior_v.at[pl.ds(0, E - 1)], one_recv.at[ST2])
@@ -340,10 +382,8 @@
     prior = prior_v[...].reshape(2 * HEAD, HEAD)
     for h in range(2):
         cols = slice(h * HEAD, (h + 1) * HEAD)
-        entering = jnp.exp(-rates[h] * (place + 1.0))
-        attended = (
-            inside_v[:, cols] + mm(q_ref[:, cols], prior[h * HEAD : (h + 1) * HEAD]) * entering
-        )
+        outside = mm(q_ref[:, cols], prior[h * HEAD : (h + 1) * HEAD])
+        attended = inside_v[:, cols] + outside * enter_v[:, cols]
         scale = lax.rsqrt(jnp.mean(attended * attended, axis=1, keepdims=True) + 1e-06)
         ho_v[:, cols] = (attended * scale * open_v[:, cols]).astype(BF)
 
@@ -415,28 +455,24 @@
 
         def send_rows(i, carry):
             to = everyone(i)
+            slot = slot_at(to)
+            group = sum((slot >= r).astype(jnp.int32) for r in reach[1:-1])
             put(
                 mst_v.at[lax.div(to, 2)],
-                arr_v.at[mine],
+                arr_v.at[slot],
                 one_send.at[DISP],
-                one_recv.at[DISP],
+                disp_recv.at[group],
                 to,
                 t,
             )
             return carry
 
         lax.fori_loop(0, C - 1, send_rows, 0)
-        arr_v[mine] = mst_v[mine]
-        wait_bytes(arr_v.at[pl.ds(0, E - 1)], one_recv.at[DISP])
-
-    pl.when(idle)(functools.partial(wait_bytes, arr_v, one_recv.at[DISP]))
+        arr_v[own_slot] = mst_v[mine]
+
     for _ in range(2):
         later(mst_v.at[pl.ds(0, E - 1)], one_send.at[DISP], active)
     later(mst_v.at[0], one_send.at[DISP], active)
-
-    spread = mm(spread_v[...], arr_v[...].reshape(E * MSG, LANE)).astype(BF)
-    for l in range(TILES):
-        x_v[z, :, l * LANE : (l + 1) * LANE] = spread[l * RQ : (l + 1) * RQ]
 
     def at_z(step):
         return lax.rem(z + step + 2 * NZ, NZ)
@@ -460,120 +496,163 @@
         )
         later(piece, ag_send.at[way, step - 1, p])
 
-    def take(step):
+    def take(step, p=None):
         chunk = at_z(step)
-        rows = pl.ds(pl.multiple_of(chunk * SLAB, SLAB), SLAB)
-        x = x_v[chunk]
-        new = mm_nt(x, w1_v[:, rows])
-        wide = x.astype(F32) / gain_ref[rows].reshape(1, SLAB)
+        cols = pl.ds(pl.multiple_of(chunk * SLAB, SLAB), SLAB)
+        begin, size = (0, RQ) if p is None else parts[p]
+        rows = pl.ds(begin, size)
+        x = x_v[chunk, rows]
+        new = mm_nt(x, w1_v[:, cols])
+        wide = x.astype(F32) * (1.0 / gain_ref[cols].reshape(1, SLAB))
         wide = wide * wide
         squares = wide[:, :LANE]
         for l in range(1, TILES):
             squares = squares + wide[:, l * LANE : (l + 1) * LANE]
         if step == 0:
-            sum_v[...] = new
-            square_v[...] = squares
+            sum_v[rows] = new
+            square_v[rows] = squares
+        elif p is None:
+            sum_v[rows] += new
+            square_v[rows] += squares
         else:
-            sum_v[...] += new
-            square_v[...] += squares
-
-    for p in range(count):
+            return sum_v[rows] + new, square_v[rows] + squares
+
+    def down(step, hidden):
+        cols = pl.ds(pl.multiple_of(at_z(step) * SLAB, SLAB), SLAB)
+        return mm(hidden, wd_v[:, cols])
+
+    def add_up(step, way, p, value):
+        begin, size = parts[p]
+        piece = pl.ds(begin, size)
+        sp_v[way, step - 1, piece] = value.astype(BF)
+        put(
+            sp_v.at[way, step - 1, piece],
+            rp_v.at[way, step - 1, piece],
+            rs_send.at[way, step - 1, p],
+            rs_recv.at[way, step - 1, p],
+            c,
+            2 * at_z(1 - 2 * way) + core,
+        )
+        later(sp_v.at[way, step - 1, piece], rs_send.at[way, step - 1, p])
+
+    for p, (begin, size) in enumerate(parts):
+        low, high = reach[p], reach[p + 1]
+        if low < high:
+            if p == 0:
+                pl.when(active)(
+                    functools.partial(
+                        wait_bytes, arr_v.at[pl.ds(0, high - 1)], disp_recv.at[0]
+                    )
+                )
+                pl.when(idle)(
+                    functools.partial(wait_bytes, arr_v.at[pl.ds(0, high)], disp_recv.at[0])
+                )
+            else:
+                wait_bytes(arr_v.at[pl.ds(low, high - low)], disp_recv.at[p])
+        deep = MSG * (high - begins[p])
+        if deep:
+            rows = arr_v[begins[p] : high].reshape(deep, LANE)
+            start = TILES * begin
+            spread = mm(spread_v[start : start + TILES * size, :deep], rows).astype(BF)
+            for l in range(TILES):
+                x_v[z, begin : begin + size, l * LANE : (l + 1) * LANE] = spread[
+                    l * size : (l + 1) * size
+                ]
+        else:
+            x_v[z, begin : begin + size] = jnp.zeros((size, SLAB), BF)
         for way in range(2):
             if p in carried(1, way):
                 pass_on(1, way, p)
     have(1)
     have(2)
     ready = [0]
-    for step in range(1, H + 1):
+    for step in range(1, H):
         for p in range(count):
             for way in range(2):
-                if p in carried(step, way):
-                    begin, size = parts[p]
-                    wait_bytes(
-                        x_v.at[at_z((2 * way - 1) * step), pl.ds(begin, size)],
-                        ag_recv.at[way, step - 1, p],
-                    )
-                    if step < H and p in carried(step + 1, way):
-                        pass_on(step + 1, way, p)
+                begin, size = parts[p]
+                wait_bytes(
+                    x_v.at[at_z((2 * way - 1) * step), pl.ds(begin, size)],
+                    ag_recv.at[way, step - 1, p],
+                )
+                if p in carried(step + 1, way):
+                    pass_on(step + 1, way, p)
             if ready:
                 take(ready.pop(0))
         while ready:
             take(ready.pop(0))
-        ready = [-step, step] if step < H else [H]
-    take(H)
-
-    inverse = lax.rsqrt(jnp.sum(square_v[...], axis=1, keepdims=True) / D + 1e-05)
-    gate = sum_v[:, : 2 * UNITS] * inverse
-    up = sum_v[:, 2 * UNITS :] * inverse
-    hidden = (jax.nn.silu(gate) * up).astype(BF)
+        ready = [-step, step]
+    while ready:
+        take(ready.pop(0))
     have(3)
 
-    def down(step):
-        cols = pl.ds(pl.multiple_of(at_z(step) * SLAB, SLAB), SLAB)
-        return mm(hidden, wd_v[:, cols])
-
-    for step in range(1, H + 1):
-        if step == 1:
-            far = down(H)
-            values = (far, far)
-        else:
-            values = (down(H + 1 - step), down(-(H + 1 - step)))
+    for p in sorted(range(count), key=lambda p: p if p < split else p - split + 0.5):
+        way = 0 if p < split else 1
+        begin, size = parts[p]
+        wait_bytes(x_v.at[at_z(H), pl.ds(begin, size)], ag_recv.at[way, H - 1, p])
+        sums, squares = take(H, p)
+        inverse = lax.rsqrt(jnp.sum(squares, axis=1, keepdims=True) / D + 1e-05)
+        gate = sums[:, : 2 * UNITS] * inverse
+        up = sums[:, 2 * UNITS :] * inverse
+        hidden = (jax.nn.silu(gate) * up).astype(BF)
+        hidden_v[begin : begin + size] = hidden
+        add_up(1, way, p, down(H, hidden))
+
+    for step in range(2, H + 1):
+        values = (down(H + 1 - step, hidden_v[...]), down(step - H - 1, hidden_v[...]))
         for p in range(count):
             begin, size = parts[p]
             piece = pl.ds(begin, size)
             for way in range(2):
-                if step == 1 and p not in carried(H, way):
-                    continue
                 value = values[way][begin : begin + size]
-                if step > 2 or (step == 2 and p in carried(H, way)):
+                if step > 2 or p in carried(H, way):
                     wait_bytes(rp_v.at[way, step - 2, piece], rs_recv.at[way, step - 2, p])
                     value = value + rp_v[way, step - 2, piece].astype(F32)
-                sp_v[way, step - 1, piece] = value.astype(BF)
-                put(
-                    sp_v.at[way, step - 1, piece],
-                    rp_v.at[way, step - 1, piece],
-                    rs_send.at[way, step - 1, p],
-                    rs_recv.at[way, step - 1, p],
-                    c,
-                    2 * at_z(1 - 2 * way) + core,
-                )
-                later(sp_v.at[way, step - 1, piece], rs_send.at[way, step - 1, p])
-    own = down(0)
-    pieces = []
-    for p in range(count):
-        begin, size = parts[p]
+                add_up(step, way, p, value)
+
+    own = down(0, hidden_v[...])
+
+    def send_back(slot, carry):
+        @pl.when(jnp.logical_not(active & (slot == own_slot)))
+        def _():
+            put(
+                m2_v.at[slot],
+                ret_v.at[c],
+                one_send.at[RETN],
+                one_recv.at[RETN],
+                block_of(slot),
+                t,
+            )
+
+        return carry
+
+    for p, (begin, size) in enumerate(parts):
         piece = pl.ds(begin, size)
         value = own[begin : begin + size]
         for way in range(2):
             if H > 1 or p in carried(H, way):
                 wait_bytes(rp_v.at[way, H - 1, piece], rs_recv.at[way, H - 1, p])
                 value = value + rp_v[way, H - 1, piece].astype(F32)
-        pieces.append(value.astype(BF))
-    final = jnp.concatenate(pieces, axis=0)
-
-    message = jnp.zeros((E * MSG, LANE), F32)
-    for l in range(TILES):
-        message = message + mm(gather_v[l], final[:, l * LANE : (l + 1) * LANE])
-    m2_v[...] = message.astype(BF).reshape(E, MSG, LANE)
-
-    def send_back(i, carry):
-        j = pairs(i)
-        put(m2_v.at[j], ret_v.at[c], one_send.at[RETN], one_recv.at[RETN], 2 * j + core, t)
-        return carry
-
-    lax.fori_loop(0, E - 1, send_back, 0)
-
-    @pl.when(idle)
-    def _():
-        send_back(E - 1, 0)
-
+        last_v[piece] = value.astype(BF)
+        low, high = whole[p], whole[p + 1]
+        if low < high:
+            base = CAP * low // 16 * 16
+            deep = edges[p + 1] - base
+            message = jnp.zeros((MSG * (high - low), LANE), F32)
+            for l in range(TILES):
+                message = message + mm(
+                    gather_v[l, MSG * low : MSG * high, :deep],
+                    last_v[base : base + deep, l * LANE : (l + 1) * LANE],
+                )
+            m2_v[low:high] = message.astype(BF).reshape(high - low, MSG, LANE)
+            lax.fori_loop(low, high, send_back, 0)
+    finish()
     later(m2_v.at[pl.ds(0, E - 1)], one_send.at[RETN], active)
     later(m2_v, one_send.at[RETN], idle)
     width = out_ref.shape[1]
 
     @pl.when(active)
     def _():
-        ret_v[c] = m2_v[mine]
+        ret_v[c] = m2_v[own_slot]
         wait_bytes(ret_v.at[pl.ds(0, C - 1)], one_recv.at[RETN])
         tall = mm(comb_v[...], ret_v[...].reshape(C * MSG, LANE))
         moe = jnp.concatenate([tall[l * TOK : (l + 1) * TOK] for l in range(TILES)], axis=1)
@@ -622,6 +701,7 @@
             pltpu.VMEM((E, PR, HEAD), BF),
             pltpu.VMEM((TOK, 2 * HEAD), F32),
             pltpu.VMEM((TOK, 2 * HEAD), F32),
+            pltpu.VMEM((TOK, 2 * HEAD), F32),
             pltpu.VMEM((TOK, 2 * HEAD), BF),
             pltpu.VMEM((TOK, 2 * HEAD), BF),
             pltpu.VMEM((NZ, TOK, WIDE), BF),
@@ -636,6 +716,8 @@
             pltpu.VMEM((NZ, RQ, SLAB), BF),
             pltpu.VMEM((RQ, 4 * UNITS), F32),
             pltpu.VMEM((RQ, LANE), F32),
+            pltpu.VMEM((RQ, 2 * UNITS), BF),
+            pltpu.VMEM((RQ, SLAB), BF),
             pltpu.VMEM((2, H, RQ, SLAB), BF),
             pltpu.VMEM((2, H, RQ, SLAB), BF),
             pltpu.VMEM((E, MSG, LANE), BF),
@@ -647,6 +729,7 @@
             dma((4,)),
             dma((8,)),
             dma((8,)),
+            dma((PARTS,)),
             dma((2, H, PARTS)),
             dma((2, H, PARTS)),
             dma((2, H, PARTS)),

time: 87.5 us -> 84.7 us (0.968)
  Pallas kernels: 85.9 us -> 83.2 us
    pallas_call x1, Pallas kernels: 85.9 us -> 83.2 us  [local(): pl.pallas_call(functools.partial(kernel, C, NT, tokens), out_shape=jax.Sh...]
where the time goes in v3:
time: 84.7 us; the launch traced here: 84.6 us
  Pallas kernels  83.2 us (98%)
  local copies, waits for them, and re-layouts  1.38 us (2%)
    pallas_call x1, Pallas kernels, local(): pl.pallas_call(functools.partial(kernel, C, NT, tokens), out_shape=jax.Sh...  83.2 us

profile of v3, /device:TPU:1, one launch (start us, length us, event | category | flops | bytes accessed | tf_op | source)
XLA Modules:
  0.0 84.6 jit_solution(7799599120780849674)
XLA Ops:
  0.0 83.2 %layer.1 = bf16[64,192]{1,0:T(8,128)(2,1)} custom-call(s32[2]{0:T(128)} %idx_ref.1, bf16[64,256]{1,0:T(8,128)(2,1)} %q_hbm.1, bf16[64,256]{1,0:T(8,128)(2,1)} %k_hbm.1, bf16[64,256]{1,0:T(8,128)(2,1)} %v_hbm.1, bf16[64,256]{1,0:T(8,128)(2,1)} %og_hbm.1, f32[3072]{0:T(1024)} %gain_hbm.1, s32[2,64]{1,0:T(2,128)} %bitcast.6, s32[2,64]{1,0:T(2,128)} %bitcast.7, ...), custom_call_target="tpu_custom_call" | custom-call | flops 1000000000 | bytes 8000000 | tf_op jit(solution)/shard_map/layer/pallas_call | solution.py:682
  83.2 1.4 %copy.14 = bf16[64,192]{1,0:T(8,128)(2,1)} copy(bf16[64,192]{1,0:T(8,128)(2,1)} %layer.1) | data formatting | bytes 49152

commit v4 on v3

--- a/solution.py
+++ b/solution.py
@@ -18,7 +18,7 @@
 MSG = 32
 UNITS = 144
 WIDE = 256
-PARTS = 4
+PARTS = 3
 NX = 4
 MESH = pl.DeviceIdType.MESH
 BF = jnp.bfloat16
@@ -140,33 +140,22 @@
     y_at = lax.div(c, NX)
     x_at = lax.rem(c, NX)
 
-    def away(k, n):
-        half = lax.div(k + 1, 2)
-        return lax.rem(n // 2 + jnp.where(lax.rem(k, 2) == 1, n - half, half), n)
-
-    def everyone(i):
-        to_y = lax.rem(y_at + away(lax.div(i, NX), NY), NY)
-        return NX * to_y + lax.rem(x_at + away(lax.rem(i, NX), NX), NX)
-
-    def pairs(i):
-        hop = NX // 2 - 1 - lax.rem(i, NX // 2)
-        to_y = lax.rem(y_at + away(lax.div(i, NX // 2), NY), NY)
-        return NX // 2 * to_y + lax.rem(lax.div(x_at, 2) + hop, NX // 2)
-
-    def slot_at(to):
-        far = lax.rem(y_at - lax.div(to, NX) + NY, NY)
-        rank = jnp.where(
-            far == 0, 0, jnp.where(far <= NY // 2, 2 * far - 1, 2 * (NY - far))
-        )
-        return NX // 2 * rank + lax.div(x_at, 2)
-
-    def block_of(slot):
-        rank = lax.div(slot, NX // 2)
-        half = lax.div(rank + 1, 2)
-        far = jnp.where(lax.rem(rank, 2) == 1, half, NY - half)
-        return NX * lax.rem(y_at + far, NY) + core + 2 * lax.rem(slot, NX // 2)
-
-    own_slot = lax.div(x_at, 2)
+    def falling(n):
+        return sorted(range(n), key=lambda d: -min(d, n - d))
+
+    def rank(d):
+        return 0 if d == 0 else 2 * d - 1 if d <= NY // 2 else 2 * (NY - d)
+
+    at_y = [lax.rem(y_at + d, NY) for d in range(NY)]
+    at_x = [lax.rem(x_at + d, NX) for d in range(NX)]
+    pair_x = [lax.div(x, 2) for x in at_x]
+    slabs = [lax.rem(z + d, NZ) for d in range(NZ)]
+    everyone = [(dy, dx) for dy in falling(NY) for dx in falling(NX)][:-1]
+
+    def ctx_at(dy, dx):
+        return NX * at_y[dy] + at_x[dx]
+
+    own_slot = pair_x[0]
 
     ST1, ST2, HO, RS, PAIR, DISP, RETN, FIN = range(8)
 
@@ -210,20 +199,35 @@
 
     barrier = pltpu.get_barrier_semaphore()
 
-    def greet_ctx(i, carry):
+    def greet(ctx, tp):
         pl.semaphore_signal(
-            barrier, inc=1, device_id={"ctx": everyone(i), "tp": t}, device_id_type=MESH
+            barrier, inc=1, device_id={"ctx": ctx, "tp": tp}, device_id_type=MESH
         )
-        return carry
-
-    def greet_tp(i, carry):
-        pl.semaphore_signal(
-            barrier, inc=1, device_id={"ctx": c, "tp": lax.rem(t + i, NT)}, device_id_type=MESH
-        )
-        return carry
-
-    lax.fori_loop(0, C - 1, greet_ctx, 0)
-    lax.fori_loop(1, NT, greet_tp, 0)
+
+    def beside(dz):
+        return 2 * slabs[dz] + 1 - side
+
+    ring_peers = sorted({1, 2 % NZ, NZ - 2, NZ - 1} - {0})
+
+    for dy, dx in everyone:
+        if dx % 2:
+            greet(ctx_at(dy, dx), t)
+    for dz in range(1, NZ):
+        greet(c, 2 * slabs[dz] + side)
+
+    @pl.when(active)
+    def _():
+        for dy, dx in everyone:
+            if dx % 2 == 0:
+                greet(ctx_at(dy, dx), t)
+        for dz in range(NZ):
+            greet(c, beside(dz))
+
+    @pl.when(idle)
+    def _():
+        greet(c, sib)
+        for dz in ring_peers:
+            greet(c, beside(dz))
 
     def rows_of(ref, n):
         return ref.at[pl.ds(n * UNITS, UNITS)]
@@ -259,20 +263,31 @@
         each = HEAD // PR
         state_v[h * each : (h + 1) * each] = state.reshape(each, PR, HEAD)
 
-    pl.semaphore_wait(barrier, C - 1 + NT - 1)
-
-    def send_piece(i, carry):
-        j = pairs(i)
-        put(
-            state_v.at[j], win_v.at[c], one_send.at[ST1], one_recv.at[ST1], 2 * j + core, t
-        )
-        return carry
-
-    lax.fori_loop(0, E - 1, send_piece, 0)
+    @pl.when(active)
+    def _():
+        pl.semaphore_wait(barrier, C - 1 + NT - 1)
 
     @pl.when(idle)
     def _():
-        send_piece(E - 1, 0)
+        pl.semaphore_wait(barrier, E + NZ + len(ring_peers))
+
+    def to_pair(dy, k):
+        half = lax.rem(own_slot + k, NX // 2)
+        j = NX // 2 * at_y[dy] + half
+        return j, 2 * j + core
+
+    far_pairs = [(dy, k) for dy in falling(NY) for k in falling(NX // 2)]
+
+    def send_piece(dy, k):
+        j, to = to_pair(dy, k)
+        put(state_v.at[j], win_v.at[c], one_send.at[ST1], one_recv.at[ST1], to, t)
+
+    for dy, k in far_pairs[:-1]:
+        send_piece(dy, k)
+
+    @pl.when(idle)
+    def _():
+        send_piece(0, 0)
 
     later(state_v.at[pl.ds(0, E - 1)], one_send.at[ST1], active)
     later(state_v, one_send.at[ST1], idle)
@@ -313,12 +328,9 @@
 
         lax.fori_loop(0, C, turn, jnp.zeros((PR, HEAD), F32), unroll=True)
 
-        def send_prefix(i, carry):
-            to = everyone(i)
+        for dy, dx in everyone:
+            to = ctx_at(dy, dx)
             put(pst_v.at[to], prior_v.at[mine], one_send.at[ST2], one_recv.at[ST2], to, t)
-            return carry
-
-        lax.fori_loop(0, C - 1, send_prefix, 0)
         prior_v[mine] = pst_v[c]
 
     later(pst_v.at[pl.ds(0, C - 1)], one_send.at[ST2], active)
@@ -398,7 +410,7 @@
     def project(begin, size):
         lanes = pl.ds(begin, size)
         for i in order:
-            zz = lax.rem(z + i, NZ)
+            zz = slabs[i]
             cols = pl.ds(pl.multiple_of(zz * SLAB, SLAB) + begin, size)
             part = mm(ho_v[...], wout_v[0, :, cols]) + mm(hs_v[...], wout_v[1, :, cols])
             rst_v[i, :, :size] = part.astype(BF)
@@ -453,21 +465,20 @@
         )
         mst_v[...] = mm(pick_v[...], stacked).astype(BF).reshape(E, MSG, LANE)
 
-        def send_rows(i, carry):
-            to = everyone(i)
-            slot = slot_at(to)
-            group = sum((slot >= r).astype(jnp.int32) for r in reach[1:-1])
+        for dy, dx in everyone:
+            first = NX // 2 * rank((NY - dy) % NY)
+            groups = [sum(first + k >= r for r in reach[1:-1]) for k in range(NX // 2)]
+            group = groups[0]
+            for k in range(1, NX // 2):
+                group = group + (groups[k] - groups[k - 1]) * lax.div(own_slot, k)
             put(
-                mst_v.at[lax.div(to, 2)],
-                arr_v.at[slot],
+                mst_v.at[NX // 2 * at_y[dy] + pair_x[dx]],
+                arr_v.at[first + own_slot],
                 one_send.at[DISP],
                 disp_recv.at[group],
-                to,
+                ctx_at(dy, dx),
                 t,
             )
-            return carry
-
-        lax.fori_loop(0, C - 1, send_rows, 0)
         arr_v[own_slot] = mst_v[mine]
 
     for _ in range(2):
@@ -475,26 +486,30 @@
     later(mst_v.at[0], one_send.at[DISP], active)
 
     def at_z(step):
-        return lax.rem(z + step + 2 * NZ, NZ)
+        return slabs[step % NZ]
 
     def carried(step, way):
         if step < H:
             return range(count)
         return range(split) if way == 0 else range(split, count)
 
-    def pass_on(step, way, p):
+    def pass_on(step, hops, way, n, p):
         turn = 1 - 2 * way
         begin, size = parts[p]
-        piece = x_v.at[at_z(-turn * (step - 1)), pl.ds(begin, size)]
+        piece = x_v.at[at_z(step), pl.ds(begin, size)]
         put(
             piece,
             piece,
-            ag_send.at[way, step - 1, p],
-            ag_recv.at[way, step - 1, p],
+            ag_send.at[way, n, p],
+            ag_recv.at[way, n, p],
             c,
-            2 * at_z(turn) + core,
+            2 * at_z(turn * hops) + core,
         )
-        later(piece, ag_send.at[way, step - 1, p])
+        later(piece, ag_send.at[way, n, p])
+
+    def landed(step, way, n, p):
+        begin, size = parts[p]
+        wait_bytes(x_v.at[at_z(step), pl.ds(begin, size)], ag_recv.at[way, n, p])
 
     def take(step, p=None):
         chunk = at_z(step)
@@ -560,29 +575,41 @@
                 ]
         else:
             x_v[z, begin : begin + size] = jnp.zeros((size, SLAB), BF)
-        for way in range(2):
-            if p in carried(1, way):
-                pass_on(1, way, p)
+        for hops in (2, 1) if H == 4 else (1,):
+            for way in range(2):
+                if p in carried(hops, way):
+                    pass_on(0, hops, way, hops - 1, p)
     have(1)
     have(2)
     ready = [0]
-    for step in range(1, H):
+    if H == 4:
         for p in range(count):
             for way in range(2):
-                begin, size = parts[p]
-                wait_bytes(
-                    x_v.at[at_z((2 * way - 1) * step), pl.ds(begin, size)],
-                    ag_recv.at[way, step - 1, p],
-                )
-                if p in carried(step + 1, way):
-                    pass_on(step + 1, way, p)
-            if ready:
+                back = 4 * way - 2
+                landed(back, way, 1, p)
+                if p in carried(H, way):
+                    pass_on(back, 2, way, 3, p)
+                pass_on(back, 1, way, 2, p)
+        take(0)
+        for n in (0, 1, 2):
+            if n != 1:
+                for p in range(count):
+                    for way in range(2):
+                        landed((2 * way - 1) * (n + 1), way, n, p)
+            take(n + 1)
+            take(-n - 1)
+    else:
+        for step in range(1, H):
+            for p in range(count):
+                for way in range(2):
+                    landed((2 * way - 1) * step, way, step - 1, p)
+                    if p in carried(step + 1, way):
+                        pass_on((2 * way - 1) * step, 1, way, step, p)
+            while ready:
                 take(ready.pop(0))
+            ready = [-step, step]
         while ready:
             take(ready.pop(0))
-        ready = [-step, step]
-    while ready:
-        take(ready.pop(0))
     have(3)
 
     for p in sorted(range(count), key=lambda p: p if p < split else p - split + 0.5):
@@ -611,19 +638,19 @@
 
     own = down(0, hidden_v[...])
 
-    def send_back(slot, carry):
-        @pl.when(jnp.logical_not(active & (slot == own_slot)))
-        def _():
-            put(
-                m2_v.at[slot],
-                ret_v.at[c],
-                one_send.at[RETN],
-                one_recv.at[RETN],
-                block_of(slot),
-                t,
-            )
-
-        return carry
+    by_rank = sorted(range(NY), key=rank)
+
+    def send_back(slot):
+        dy, k = by_rank[slot // (NX // 2)], slot % (NX // 2)
+        to = NX * at_y[dy] + 2 * k + core
+
+        def go():
+            put(m2_v.at[slot], ret_v.at[c], one_send.at[RETN], one_recv.at[RETN], to, t)
+
+        if dy:
+            go()
+        else:
+            pl.when(jnp.logical_not(active & (own_slot == k)))(go)
 
     for p, (begin, size) in enumerate(parts):
         piece = pl.ds(begin, size)
@@ -644,7 +671,8 @@
                     last_v[base : base + deep, l * LANE : (l + 1) * LANE],
                 )
             m2_v[low:high] = message.astype(BF).reshape(high - low, MSG, LANE)
-            lax.fori_loop(low, high, send_back, 0)
+            for slot in reversed(range(low, high)):
+                send_back(slot)
     finish()
     later(m2_v.at[pl.ds(0, E - 1)], one_send.at[RETN], active)
     later(m2_v, one_send.at[RETN], idle)

time: 84.7 us -> 84.2 us (level)
  no operation moved by 1% of the time
where the time goes in v4:
time: 84.2 us; the launch traced here: 83.9 us
  Pallas kernels  82.6 us (98%)
  local copies, waits for them, and re-layouts  1.38 us (2%)
    pallas_call x1, Pallas kernels, local(): pl.pallas_call(functools.partial(kernel, C, NT, tokens), out_shape=jax.Sh...  82.6 us

profile of v4, /device:TPU:1, one launch (start us, length us, event | category | flops | bytes accessed | tf_op | source)
XLA Modules:
  0.0 83.9 jit_solution(13570740170002423779)
XLA Ops:
  0.0 82.6 %layer.1 = bf16[64,192]{1,0:T(8,128)(2,1)} custom-call(s32[2]{0:T(128)} %idx_ref.1, bf16[64,256]{1,0:T(8,128)(2,1)} %q_hbm.1, bf16[64,256]{1,0:T(8,128)(2,1)} %k_hbm.1, bf16[64,256]{1,0:T(8,128)(2,1)} %v_hbm.1, bf16[64,256]{1,0:T(8,128)(2,1)} %og_hbm.1, f32[3072]{0:T(1024)} %gain_hbm.1, s32[2,64]{1,0:T(2,128)} %bitcast.6, s32[2,64]{1,0:T(2,128)} %bitcast.7, ...), custom_call_target="tpu_custom_call" | custom-call | flops 1000000000 | bytes 8000000 | tf_op jit(solution)/shard_map/layer/pallas_call | solution.py:710
  82.6 1.4 %copy.14 = bf16[64,192]{1,0:T(8,128)(2,1)} copy(bf16[64,192]{1,0:T(8,128)(2,1)} %layer.1) | data formatting | bytes 49152
